TPU v7x, 128 devices: a whole 4x4x4 slice. The times are simulated.
128 devices in a mesh: node: 16 (over y, x), local: 8 (over z, core).
Axes of the slice: x: 4, y: 4, z: 4, core: 2. Of those that a mesh axis runs over, the one named last changes fastest.
Arguments:
- hidden_in: bfloat16 [1024, 7168], P(('node', 'local')), may hold values from -6 to 6
- expert_ids: int32 [1024, 8], P(('node', 'local')), may hold values from 0 to 31, all different within a row; in each aligned block of 64 rows (0 to 63, 64 to 127, ...) at most 24 rows name the same one
- affinity: bfloat16 [1024, 8], P(('node', 'local')), may hold values from 0.049804688 to 1
- norm_gain: float32 [7168], replicated, may hold values from 0.5 to 1.5
- gate_w: bfloat16 [128, 7168, 512], P(('node', 'local')), may hold values from -0.0625 to 0.0625
- up_w: bfloat16 [128, 7168, 512], P(('node', 'local')), may hold values from -0.0625 to 0.0625
- down_w: bfloat16 [32, 2048, 7168], P('node', None, 'local'), may hold values from -0.125 to 0.125
- shared_gate: bfloat16 [7168, 2048], P(None, 'local'), may hold values from -0.0625 to 0.0625
- shared_up: bfloat16 [7168, 2048], P(None, 'local'), may hold values from -0.0625 to 0.0625
- shared_down: bfloat16 [2048, 7168], P(None, 'local'), may hold values from -0.125 to 0.125
Outputs:
- block_out: bfloat16 [1024, 7168], P('node', 'local')
Inputs may be any that keep to these rules, and one draw needn't show every extreme that they name: `expert_ids`: each token names 8 different experts; in each aligned block of 64 tokens no expert is named more than 24 times, a bound that some block reaches.
All inputs are finite; a program needn't handle non-finite values.
Results may differ from a plain program's by a relative error of at most 0.0055.
Values may be sent and summed in bfloat16 or wider, within the bound.
A program may use at most 128 MiB of HBM per device.

v0:
```python
import jax
import jax.numpy as jnp
from jax import lax
from jax.sharding import PartitionSpec as P


def body(
    hidden_in,
    expert_ids,
    affinity,
    norm_gain,
    gate_w,
    up_w,
    down_w,
    shared_gate,
    shared_up,
    shared_down,
):
    node_count = lax.axis_size("node")
    local_count = lax.axis_size("local")
    width = hidden_in.shape[1]
    col_width = width // local_count
    e_node = down_w.shape[0]
    expert_count = e_node * node_count
    hidden_parts = local_count // e_node
    own_expert = lax.axis_index("local") // hidden_parts
    values = hidden_in.astype(jnp.float32)
    scale = lax.rsqrt(jnp.mean(values * values, axis=-1, keepdims=True) + 1e-06)
    normed = (values * scale * norm_gain).astype(jnp.bfloat16)
    node_rows, node_aff = (
        lax.all_gather(normed, "local", axis=0, tiled=True),
        lax.all_gather(affinity, "local", axis=0, tiled=True),
    )
    node_ids = lax.all_gather(expert_ids, "local", axis=0, tiled=True)
    resid_cols = lax.all_to_all(hidden_in, "local", split_axis=1, concat_axis=0, tiled=True)
    block_rows = node_rows.shape[0]
    top_count = node_ids.shape[1]
    capacity = min(block_rows, 3 * block_rows * top_count // (2 * expert_count))
    slot_rows = node_count * capacity
    flat_ids = node_ids.reshape(-1)
    onehot = (flat_ids[:, None] == jnp.arange(expert_count, dtype=jnp.int32)[None, :]).astype(
        jnp.int32
    )
    before = jnp.cumsum(onehot, axis=0) - onehot
    slot_index = jnp.sum(before * onehot, axis=1)
    target = flat_ids * capacity + slot_index
    row_of = jnp.arange(block_rows * top_count, dtype=jnp.int32) // top_count
    spread_rows = node_rows[row_of]
    buffer = jnp.zeros((expert_count * capacity, width), jnp.bfloat16).at[target].set(spread_rows)
    buffer = buffer.reshape(node_count, e_node, capacity, width)
    arrived = lax.all_to_all(buffer, "node", split_axis=0, concat_axis=2, tiled=True)
    mine = lax.dynamic_index_in_dim(arrived, own_expert, 1, keepdims=False).reshape(
        slot_rows, width
    )
    gate = jnp.dot(mine, gate_w[0], preferred_element_type=jnp.float32)
    upper = jnp.dot(mine, up_w[0], preferred_element_type=jnp.float32)
    act = (jax.nn.silu(gate) * upper).astype(jnp.bfloat16)
    shared_g = jnp.dot(node_rows, shared_gate, preferred_element_type=jnp.float32)
    shared_u = jnp.dot(node_rows, shared_up, preferred_element_type=jnp.float32)
    shared_act = (jax.nn.silu(shared_g) * shared_u).astype(jnp.bfloat16)
    act_all, shared_all = (
        lax.all_gather(act, "local", axis=1, tiled=True),
        lax.all_gather(shared_act, "local", axis=1, tiled=True),
    )
    act_all = act_all.reshape(slot_rows, e_node, down_w.shape[1])
    routed_term = jnp.einsum("rep,epd->erd", act_all, down_w, preferred_element_type=jnp.float32)
    routed_term = routed_term.astype(jnp.bfloat16).reshape(e_node, node_count, capacity, col_width)
    shared_sum = jnp.dot(shared_all, shared_down, preferred_element_type=jnp.float32)
    returned = lax.all_to_all(routed_term, "node", split_axis=1, concat_axis=0, tiled=True)
    returned = returned.reshape(expert_count * capacity, col_width)
    picked = returned[target].astype(jnp.float32).reshape(block_rows, top_count, col_width)
    weight_in = node_aff.astype(jnp.float32)
    mix = 2.5 * weight_in / jnp.sum(weight_in, axis=-1, keepdims=True)
    routed = jnp.sum(mix[:, :, None] * picked, axis=1)
    return (resid_cols.astype(jnp.float32) + shared_sum + routed).astype(jnp.bfloat16)


def solution(mesh):
    in_specs = (
        P(("node", "local"), None),
        P(("node", "local"), None),
        P(("node", "local"), None),
        P(),
        P(("node", "local"), None, None),
        P(("node", "local"), None, None),
        P("node", None, "local"),
        P(None, "local"),
        P(None, "local"),
        P(None, "local"),
    )
    out_specs = P("node", "local")
    return jax.shard_map(body, mesh=mesh, in_specs=in_specs, out_specs=out_specs, check_vma=False)
```

profile of v0, /device:TPU:0, one launch (start us, length us, event | category | flops | bytes accessed | tf_op | source)
XLA Modules:
  0.0 342.6 jit_solution(1302782053416637528)
XLA Ops:
  6.5 14.2 %all_gather.18 = s32[64,8]{1,0:T(8,128)S(1)} all-gather(s32[8,8]{1,0:T(8,128)} %param.11), channel_id=1, replica_groups=mesh['node'=16,'local'=8] {'local'}, dimensions={0}, use_global_device_ids=true | all-gather | bytes 2304 | tf_op jit(solution)/shard_map/all_gather | solution.py:34
  20.8 0.1 eq.29
  20.9 0.1 eq.25
  21.0 1.1 fusion.30
  22.1 0.1 mul.78
  22.2 1.2 reduce-window.6
  23.3 0.2 slice_reduce_fusion
  23.6 1.0 fusion.32
  24.6 13.5 %all_gather.15 = bf16[64,7168]{1,0:T(8,128)(2,1)S(1)} all-gather(bf16[8,7168]{1,0:T(8,128)(2,1)S(1)} %fusion.32), channel_id=1, replica_groups=mesh['node'=16,'local'=8] {'local'}, dimensions={0}, use_global_device_ids=true | all-gather | bytes 1032192 | tf_op jit(solution)/shard_map/all_gather | solution.py:31
  38.1 0.1 fusion.35
  38.2 7.0 %gather_fusion = bf16[512,7168]{1,0:T(8,128)(2,1)} fusion(bf16[64,7168]{1,0:T(8,128)(2,1)S(1)} %all_gather.15, s32[1024]{0:T(1024)S(1)} %pad_clamp_fusion.1), kind=kCustom, calls=%fused_computation | custom fusion | bytes 14682112 | tf_op jit(solution)/shard_map/gather | solution.py:48
  45.2 18.7 %scatter_custom_fusion = bf16[768,7168]{1,0:T(8,128)(2,1)} fusion(s32[512]{0:T(512)S(1)} %bitcast.79, bf16[512,7168]{1,0:T(8,128)(2,1)} %gather_fusion, bf16[]{:T(256)} %constant.55.clone.1), kind=kCustom, calls=%fused_computation.9 | custom fusion | bytes 11010560 | tf_op jit(solution)/shard_map/scatter | solution.py:49
  63.9 7.1 %all-to-all-start.1 = ((bf16[16,2,24,7168]{3,2,1,0:T(8,128)(2,1)}), bf16[16,2,24,7168]{3,2,1,0:T(8,128)(2,1)}, u32[]{:S(2)}, u32[]{:S(2)}) async-start(bf16[16,2,24,7168]{3,2,1,0:T(8,128)(2,1)} %bitcast.75), calls=%async_computation.1 | async-start | bytes 22020096 | tf_op jit(solution)/shard_map/all_to_all | solution.py:51
  71.0 0.0 all-gather.2.cloned.1.call-start
  71.1 165.5 %all-to-all-done.1 = bf16[16,2,24,7168]{3,2,1,0:T(8,128)(2,1)} async-done(((bf16[16,2,24,7168]{3,2,1,0:T(8,128)(2,1)}), bf16[16,2,24,7168]{3,2,1,0:T(8,128)(2,1)}, u32[]{:S(2)}, u32[]{:S(2)}) %all-to-all-start.1) | async-done | bytes 11010080 | tf_op jit(solution)/shard_map/all_to_all | solution.py:51
  236.6 0.0 slice-start
  236.6 6.1 %copy.21 = bf16[1,2,16,24,7168]{4,3,2,1,0:T(8,128)(2,1)S(1)} copy(bf16[1,2,16,24,7168]{4,3,1,2,0:T(8,128)(2,1)} %bitcast.9) | data formatting | bytes 22020096 | tf_op jit(solution)/shard_map/all_to_all | solution.py:51
  242.7 0.0 slice-start.1
  242.7 5.5 %fusion.2 = f32[384,512]{1,0:T(8,128)S(1)} fusion(bf16[1,7168,512]{2,1,0:T(8,128)(2,1)} %param.14, bf16[1,2,384,7168]{3,2,1,0:T(8,128)(2,1)S(1)} %bitcast.76, s32[]{:T(128)S(6)} %select_n.46), kind=kOutput, calls=%fused_computation.5 | convolution fusion | flops 2818572288 | bytes 13631492 | tf_op jit(solution)/shard_map/dot_general | solution.py:55
  248.3 0.0 slice-done
  248.3 0.0 slice-done.1
  248.3 3.8 %fusion.22 = bf16[384,512]{1,0:T(8,128)(2,1)} fusion(bf16[1,7168,512]{2,1,0:T(8,128)(2,1)S(1)} %bitcast.84, bf16[1,2,384,7168]{3,2,1,0:T(8,128)(2,1)S(1)} %bitcast.77, s32[]{:T(128)S(6)} %select_n.46, f32[384,512]{1,0:T(8,128)S(1)} %fusion.2), kind=kOutput, calls=%fused_computation.20 | convolution fusion | flops 2819751936 | bytes 14024708 | tf_op jit(solution)/shard_map/dot_general | solution.py:56
  252.1 0.0 all-gather.2.cloned.1.call-update
  252.1 25.7 %all-gather.2.cloned.1.call-done = bf16[384,4096]{1,0:T(8,128)(2,1)} async-done(((bf16[384,512]{1,0:T(8,128)(2,1)}), bf16[384,4096]{1,0:T(8,128)(2,1)}) %all-gather.2.cloned.1.call-update) | async-done | bytes 3145744 | tf_op jit(solution)/shard_map/all_gather | solution.py:62
  277.8 0.0 copy-start
  277.8 7.5 %fusion.14 = bf16[2,384,896]{2,1,0:T(8,128)(2,1)S(1)} fusion(bf16[2,2048,896]{2,1,0:T(8,128)(2,1)} %param.16, bf16[48,2,8,2048]{3,2,1,0:T(8,128)(2,1)} %bitcast.85), kind=kOutput, calls=%fused_computation.18 | convolution fusion | flops 2819260416 | bytes 11862016 | tf_op jit(solution)/shard_map/rep,epd->erd/dot_general | solution.py:66
  285.3 1.2 copy.23
  286.5 6.8 %all-to-all-start.2 = ((bf16[2,16,24,896]{3,2,0,1:T(8,128)(2,1)}), bf16[2,16,24,896]{3,2,0,1:T(8,128)(2,1)S(1)}, u32[]{:S(2)}, u32[]{:S(2)}) async-start(bf16[2,16,24,896]{3,2,0,1:T(8,128)(2,1)} %copy.23), calls=%async_computation.2 | async-start | bytes 2752512 | tf_op jit(solution)/shard_map/all_to_all | solution.py:69
  293.3 0.0 copy-done
  293.3 11.2 %all_gather.17 = bf16[64,8]{1,0:T(8,128)(2,1)S(1)} all-gather(bf16[8,8]{1,0:T(8,128)(2,1)S(1)} %copy-done), channel_id=1, replica_groups=mesh['node'=16,'local'=8] {'local'}, dimensions={0}, use_global_device_ids=true | all-gather | bytes 1152 | tf_op jit(solution)/shard_map/all_gather | solution.py:32
  304.5 0.1 convert_reduce_fusion
  304.6 2.8 fusion.40
  307.4 2.8 fusion.29
  310.2 12.8 %all_gather.16 = bf16[64,2048]{1,0:T(8,128)(2,1)S(1)} all-gather(bf16[64,256]{1,0:T(8,128)(2,1)S(1)} %fusion.29), channel_id=1, replica_groups=mesh['node'=16,'local'=8] {'local'}, dimensions={1}, use_global_device_ids=true | all-gather | bytes 294912 | tf_op jit(solution)/shard_map/all_gather | solution.py:63
  323.0 0.1 fusion.37
  323.1 0.0 all-to-all-done.2
  323.1 3.4 all-to-all-start
  326.5 2.1 gather_fusion.1
  328.6 0.6 fusion.13
  329.2 3.2 all-to-all-done
  332.4 3.4 fusion.28
  (10 shorter events, 0.1 us)
Async XLA Ops:
  63.9 172.7 %all-to-all-start.1 = ((bf16[16,2,24,7168]{3,2,1,0:T(8,128)(2,1)}), bf16[16,2,24,7168]{3,2,1,0:T(8,128)(2,1)}, u32[]{:S(2)}, u32[]{:S(2)}) async-start(bf16[16,2,24,7168]{3,2,1,0:T(8,128)(2,1)} %bitcast.75), calls=%async_computation.1 | async-start | bytes 22020096 | tf_op jit(solution)/shard_map/all_to_all | solution.py:51
  71.0 206.8 %all-gather.2.cloned.1.call-start = ((), (), s32[]{:S(2)}) async-start(), calls=%async_computation.3 | async-start | bytes 3538944 | tf_op jit(solution)/shard_map/all_gather | solution.py:62
  236.6 11.7 %slice-start = ((s8[7340032]{0:T(1024)(128)(4,1)}), s8[4194304]{0:T(1024)(128)(4,1)S(1)}, s32[]{:S(2)}) async-start(s8[7340032]{0:T(1024)(128)(4,1)} %bitcast.83), calls=%async_computation.4 | async-start | bytes 8388608
  242.7 5.6 %slice-start.1 = ((s8[7340032]{0:T(1024)(128)(4,1)}), s8[3145728]{0:T(1024)(128)(4,1)S(1)}, s32[]{:S(2)}) async-start(s8[7340032]{0:T(1024)(128)(4,1)} %bitcast.83), calls=%async_computation.5 | async-start | bytes 6291456
  277.8 15.5 %copy-start = (bf16[8,8]{1,0:T(8,128)(2,1)S(1)}, bf16[8,8]{1,0:T(8,128)(2,1)}, u32[]{:S(2)}) copy-start(bf16[8,8]{1,0:T(8,128)(2,1)} %param.12) | copy-start | bytes 388
  286.5 36.6 %all-to-all-start.2 = ((bf16[2,16,24,896]{3,2,0,1:T(8,128)(2,1)}), bf16[2,16,24,896]{3,2,0,1:T(8,128)(2,1)S(1)}, u32[]{:S(2)}, u32[]{:S(2)}) async-start(bf16[2,16,24,896]{3,2,0,1:T(8,128)(2,1)} %copy.23), calls=%async_computation.2 | async-start | bytes 2752512 | tf_op jit(solution)/shard_map/all_to_all | solution.py:69
  323.1 9.3 %all-to-all-start = ((bf16[8,8,896]{2,0,1:T(8,128)(2,1)}), bf16[8,8,896]{2,0,1:T(8,128)(2,1)S(1)}, u32[]{:S(2)}, u32[]{:S(2)}) async-start(bf16[8,8,896]{2,0,1:T(8,128)(2,1)} %bitcast), calls=%async_computation | async-start | bytes 229376 | tf_op jit(solution)/shard_map/all_to_all | solution.py:35
Sparse Core Ops, SparseCore 0:
  252.2 25.5 all-gather.1
where the time goes:
time: 344 us; the launch traced here: 343 us
  waiting for transfers between devices  194 us (56%)
  blocking collectives  51.8 us (15%)
  local copies, waits for them, and re-layouts  35.5 us (10%)
  matrix products  25.7 us (7%)
  starting transfers between devices  17.3 us (5%)
  between operations  13.6 us (4%)
  other arithmetic  4.21 us (1%)
    all_to_all x1, waiting for transfers between devices, body(): lax.all_to_all(buffer, 'node', split_axis=0, concat_axis=2, tiled=True)  166 us
    all_gather x1, waiting for transfers between devices, body(): lax.all_gather(act, 'local', axis=1, tiled=True)  25.7 us
    scatter x1, local copies, waits for them, and re-layouts, body(): jnp.zeros((expert_count * capacity, width), jnp.bfloat16).at[target]  18.7 us
    all_gather x1, blocking collectives, body(): node_ids = lax.all_gather(expert_ids, 'local', axis=0, tiled=True)  14.2 us
    all_gather x1, blocking collectives, body(): lax.all_gather(normed, 'local', axis=0, tiled=True)  13.5 us
    all_gather x1, blocking collectives, body(): lax.all_gather(shared_act, 'local', axis=1, tiled=True)  12.8 us
    all_gather x1, blocking collectives, body(): lax.all_gather(affinity, 'local', axis=0, tiled=True)  11.2 us
    dot_general x1, matrix products, body(): jnp.einsum('rep,epd->erd', act_all, down_w, preferred_element_type=jnp.fl...  7.45 us
  transfers between devices with their start and end apart: 4, of which 3 were waited for; matrix products, arithmetic and copies ran while one was open for 2% of the time, Pallas kernels for 0%

commit v1 on v0

v1 whole, which is shorter than its diff:
```python
import functools

import jax
import jax.numpy as jnp
from jax import lax
from jax.experimental import pallas as pl
from jax.experimental.pallas import tpu as pltpu
from jax.sharding import PartitionSpec as P

MESH = pl.DeviceIdType.MESH
F32 = jnp.float32
BF16 = jnp.bfloat16
RING = 4
META = 128
CAP = 24
TOP = 8


def remote(src, dst, send, recv, device):
    return pltpu.make_async_remote_copy(
        src_ref=src,
        dst_ref=dst,
        send_sem=send,
        recv_sem=recv,
        device_id=device,
        device_id_type=MESH,
    )


def dot(a, b):
    return jnp.dot(a, b, preferred_element_type=F32)


class Gather:
    def __init__(self, slot, first, second, pos, plus, minus, send, recv, other=None):
        self.slot, self.first, self.second = slot, first, second
        self.pos, self.plus, self.minus, self.other = pos, plus, minus, other
        self.send, self.recv = send, recv
        self.before = lax.rem(pos + RING - 1, RING)
        self.after = lax.rem(pos + 1, RING)
        self.far = lax.rem(pos + 2, RING)
        self.sent = []

    def copy(self, ref, index, device):
        return remote(ref, ref, self.send.at[index], self.recv.at[index], device)

    def go(self, ref, index, device):
        copy = self.copy(ref, index, device)
        copy.start()
        self.sent.append(copy)

    def share(self, place, index):
        if self.other is not None:
            self.go(self.slot(place), index, self.other)

    def start(self):
        self.go(self.slot(self.pos), 0, self.plus)
        self.go(self.slot(self.pos), 1, self.minus)
        self.share(self.pos, 4)

    def pass_on(self):
        self.copy(self.slot(self.before), 0, self.plus).wait_recv()
        self.go(self.first(self.before), 2, self.plus)
        self.copy(self.slot(self.after), 1, self.minus).wait_recv()
        self.go(self.second(self.after), 3, self.minus)
        self.share(self.before, 5)
        self.share(self.after, 6)

    def finish(self):
        self.copy(self.first(self.far), 2, self.plus).wait_recv()
        self.copy(self.second(self.far), 3, self.minus).wait_recv()
        self.share(self.far, 7)

    def shared(self, mirror):
        for place, index in ((self.pos, 4), (self.before, 5), (self.after, 6), (self.far, 7)):
            self.copy(mirror(place), index, self.other).wait_recv()

    def drain(self):
        for copy in self.sent:
            copy.wait_send()
        self.sent = []


def kernel(
    hid,
    ids,
    aff,
    gain,
    gate_hbm,
    up_hbm,
    down_hbm,
    sgate_hbm,
    sup_hbm,
    sdown_hbm,
    out,
    wg,
    wu,
    wd,
    sg,
    su,
    sd,
    pair_out,
    pair_in,
    zh,
    xa,
    xo,
    ct,
    cs,
    fw,
    rh,
    ac,
    sa,
    sres,
    oo,
    pp,
    r1,
    r2,
    t1,
    r3,
    r4,
    wsem,
    bsem,
    zsend,
    zrecv,
    asend,
    arecv,
    ssend,
    srecv,
    csend,
    crecv,
    gsend,
    grecv,
    rsend,
    rrecv,
):
    half = hid.shape[1] // 2
    node, local = lax.axis_index("node"), lax.axis_index("local")
    y, x = node // RING, lax.rem(node, RING)
    z, c = local // 2, lax.rem(local, 2)
    d = 1 - c
    up1 = lambda v: lax.rem(v + 1, RING)
    dn1 = lambda v: lax.rem(v + RING - 1, RING)
    sib = (node, z * 2 + d)
    z_plus, z_minus = (node, up1(z) * 2 + c), (node, dn1(z) * 2 + c)
    x_plus, x_minus = (y * RING + up1(x), local), (y * RING + dn1(x), local)
    y_plus, y_minus = (up1(y) * RING + x, local), (dn1(y) * RING + x, local)
    a_plus = (d * y_plus[0] + c * x_plus[0], local)
    a_minus = (d * y_minus[0] + c * x_minus[0], local)
    b_plus = (d * x_plus[0] + c * y_plus[0], local)
    b_minus = (d * x_minus[0] + c * y_minus[0], local)
    apos, bpos = d * y + c * x, d * x + c * y

    barrier = pltpu.get_barrier_semaphore()
    for peer in (sib, z_plus, z_minus, x_plus, x_minus, y_plus, y_minus):
        pl.semaphore_signal(barrier, inc=1, device_id=peer, device_id_type=MESH)

    values = hid[...].astype(F32)
    scale = lax.rsqrt(jnp.mean(values * values, axis=-1, keepdims=True) + 1e-06)
    s_hi = scale.astype(BF16).astype(F32)
    s_mid = (scale - s_hi).astype(BF16).astype(F32)
    s_lo = scale - s_hi - s_mid
    weight = aff[...].astype(F32)
    mix = 2.5 * weight / jnp.sum(weight, axis=-1, keepdims=True)
    m_hi = mix.astype(BF16).astype(F32)
    m_lo = mix - m_hi
    named = ids[...].astype(F32)
    rows = hid.shape[0]
    lane = lax.broadcasted_iota(jnp.int32, (rows, META), 1)
    place = (z * 2 * rows + c * rows + lax.broadcasted_iota(jnp.int32, (rows, META), 0)).astype(F32)
    meta = jnp.where(lane == 16, place, 0.0)
    meta = jnp.where(lane == 17, 1.0, meta)
    meta = jnp.where(lane == 18, s_hi, meta)
    meta = jnp.where(lane == 19, s_mid, meta)
    meta = jnp.where(lane == 20, s_lo, meta)
    for k in range(TOP):
        meta = jnp.where(lane == k, named[:, k : k + 1], meta)
        meta = jnp.where(lane == 8 + k, m_hi[:, k : k + 1], meta)
        meta = jnp.where(lane == 24 + k, m_lo[:, k : k + 1], meta)
    other_cols = pl.ds(pl.multiple_of(d * half, 128), half)
    own_cols = pl.ds(pl.multiple_of(c * half, 128), half)
    pair_out[:, :half] = hid[:, other_cols].astype(F32)
    pair_out[:, half:] = meta

    pl.semaphore_wait(barrier, 7)
    pair = remote(pair_out, pair_in, bsem.at[0], bsem.at[1], sib)
    pair.start()
    loads = [
        pltpu.make_async_copy(src, dst, wsem.at[i])
        for i, (src, dst) in enumerate(
            (
                (sgate_hbm, sg),
                (sup_hbm, su),
                (gate_hbm.at[0], wg),
                (up_hbm.at[0], wu),
                (sdown_hbm, sd),
                (down_hbm, wd),
            )
        )
    ]
    for load in loads:
        load.start()
    own = jnp.concatenate([hid[:, own_cols].astype(F32), meta], axis=1)
    pair.wait()
    theirs = pair_in[...]
    zh[c, z] = jnp.concatenate(
        [jnp.where(c == 0, own, theirs), jnp.where(c == 0, theirs, own)], axis=0
    ).astype(BF16)

    cut = 15 * 128
    zg = Gather(
        lambda q: zh.at[c, q],
        lambda q: zh.at[c, q, :, pl.ds(0, cut)],
        lambda q: zh.at[c, q, :, pl.ds(cut, half + META - cut)],
        z,
        z_plus,
        z_minus,
        zsend,
        zrecv,
        sib,
    )
    zg.start()
    zg.pass_on()
    zg.finish()

    block = RING * zh.shape[2]

    def normed(h):
        held = zh[h].reshape(block, half + META)
        info = held[:, half:].astype(F32)
        by = info[:, 18:19] + info[:, 19:20] + info[:, 20:21]
        return (held[:, :half].astype(F32) * by * gain[h]).astype(BF16)

    xa[apos, :, :half] = normed(c)
    xa[apos, :, half:] = zh[c, :, :, half:].reshape(block, META)
    part = block // 2
    ag = Gather(
        lambda q: xa.at[q],
        lambda q: xa.at[q, pl.ds(0, part)],
        lambda q: xa.at[q, pl.ds(part, part)],
        apos,
        a_plus,
        a_minus,
        asend,
        arecv,
    )
    ag.start()
    zg.shared(lambda q: zh.at[d, q])
    xo[...] = normed(d)

    loads[0].wait()
    loads[1].wait()
    own_rows = pl.ds(pl.multiple_of(c * half, 128), half)
    other_rows = pl.ds(pl.multiple_of(d * half, 128), half)
    mine = xa[apos, :, :half]
    s_gate = dot(mine, sg[own_rows, :]) + dot(xo[...], sg[other_rows, :])
    s_up = dot(mine, su[own_rows, :]) + dot(xo[...], su[other_rows, :])
    sa[c, z] = (s_gate / (1.0 + jnp.exp(-s_gate)) * s_up).astype(BF16)
    hrow = sa.shape[2] // 2
    sh = Gather(
        lambda q: sa.at[c, q],
        lambda q: sa.at[c, q, pl.ds(0, hrow)],
        lambda q: sa.at[c, q, pl.ds(hrow, hrow)],
        z,
        z_plus,
        z_minus,
        ssend,
        srecv,
        sib,
    )
    sh.start()
    ag.pass_on()
    sh.pass_on()
    ag.finish()

    tokens = RING * block
    info = xa[:, :, half:].reshape(tokens, META).astype(F32)
    lane = lax.broadcasted_iota(jnp.int32, (tokens, META), 1).astype(F32)
    names = jnp.zeros((tokens, META), F32)
    for k in range(TOP):
        names = jnp.where(info[:, k : k + 1] == lane, 1.0, names)
    t_row = lax.broadcasted_iota(jnp.int32, (tokens, tokens), 0)
    t_col = lax.broadcasted_iota(jnp.int32, (tokens, tokens), 1)
    earlier = jnp.where((t_col < t_row) & (t_col // block == t_row // block), 1.0, 0.0)
    counts = dot(earlier.astype(BF16), names.astype(BF16))
    base = (lax.broadcasted_iota(jnp.int32, (tokens, META), 0) // block * CAP).astype(F32)
    ct[...] = jnp.where(names > 0.5, counts + base, -1.0).T

    group = RING * CAP
    tile = 256
    tiles = half // tile
    slot_no = lax.broadcasted_iota(jnp.int32, (group, tokens), 0).astype(F32)

    def pick(step, dest):
        there = lax.rem(bpos + step, RING)
        expert = (d * (y * RING + there) + c * (there * RING + x)) * 2 + z // 2
        chosen = jnp.where(ct[pl.ds(expert, 1), :] == slot_no, 1.0, 0.0).astype(BF16)

        @pl.loop(0, tiles)
        def _(j):
            cols = pl.ds(pl.multiple_of(j * tile, tile), tile)
            dest[:, cols] = dot(chosen, xa[:, :, cols].reshape(tokens, tile)).astype(BF16)

        dest[:, half:] = dot(chosen, xa[:, :, half:].reshape(tokens, META)).astype(BF16)

    b_prev, b_next = dn1(bpos), up1(bpos)
    b_far = up1(b_next)
    gh = group // 2
    pick(2, cs.at[1])
    routed = [
        remote(cs.at[1, pl.ds(0, gh)], fw.at[0], csend.at[0], crecv.at[0], b_plus),
        remote(cs.at[1, pl.ds(gh, gh)], fw.at[1], csend.at[1], crecv.at[1], b_minus),
    ]
    routed[0].start()
    routed[1].start()
    pick(1, cs.at[0])
    routed.append(remote(cs.at[0], rh.at[c, bpos], csend.at[2], crecv.at[2], b_plus))
    routed[2].start()
    pick(3, cs.at[2])
    routed.append(remote(cs.at[2], rh.at[c, bpos], csend.at[3], crecv.at[3], b_minus))
    routed[3].start()
    pick(0, rh.at[c, bpos])

    def both(q, index):
        copy = remote(rh.at[c, q], rh.at[c, q], csend.at[index], crecv.at[index], sib)
        copy.start()
        routed.append(copy)

    both(bpos, 6)
    sh.finish()
    sh.shared(lambda q: sa.at[d, q])
    loads[4].wait()
    total = jnp.zeros(sres.shape, F32)
    wide = sa.shape[3]
    for zz in range(RING):
        for cc in range(2):
            total += dot(sa[cc, zz], sd[(zz * 2 + cc) * wide : (zz * 2 + cc + 1) * wide, :])
    sres[...] = total

    routed[0].wait_recv()
    onward = remote(
        fw.at[0], rh.at[c, b_prev, pl.ds(0, gh)], csend.at[4], crecv.at[4], b_plus
    )
    onward.start()
    routed.append(onward)
    routed[1].wait_recv()
    onward = remote(
        fw.at[1], rh.at[c, b_next, pl.ds(gh, gh)], csend.at[5], crecv.at[5], b_minus
    )
    onward.start()
    routed.append(onward)
    remote(cs.at[0], rh.at[c, b_prev], csend.at[2], crecv.at[2], b_plus).wait_recv()
    both(b_prev, 7)
    remote(cs.at[2], rh.at[c, b_next], csend.at[3], crecv.at[3], b_minus).wait_recv()
    both(b_next, 8)
    remote(
        fw.at[0], rh.at[c, b_far, pl.ds(0, gh)], csend.at[4], crecv.at[4], b_plus
    ).wait_recv()
    remote(
        fw.at[1], rh.at[c, b_far, pl.ds(gh, gh)], csend.at[5], crecv.at[5], b_minus
    ).wait_recv()
    both(b_far, 9)
    o_prev, o_next = dn1(apos), up1(apos)
    o_far = up1(o_next)
    for q, index in ((apos, 6), (o_prev, 7), (o_next, 8), (o_far, 9)):
        remote(rh.at[d, q], rh.at[d, q], csend.at[index], crecv.at[index], sib).wait_recv()

    slots = RING * group
    expert = (node * 2 + z // 2).astype(F32)
    info = rh[0, :, :, half:].reshape(slots, META).astype(F32)
    lane = lax.broadcasted_iota(jnp.int32, (slots, META), 1)
    shares = pltpu.roll(info, META - 8, 1) + pltpu.roll(info, META - 24, 1)
    factor = jnp.sum(
        jnp.where((lane < TOP) & (info == expert), shares, 0.0), axis=1, keepdims=True
    )
    s_no = lax.broadcasted_iota(jnp.int32, (slots, 1), 0)
    home = (lax.rem(s_no // CAP, RING) * block).astype(F32)
    token = jnp.where(info[:, 17:18] > 0.5, info[:, 16:17] + home, -1.0)
    for g in range(RING):
        column = jnp.broadcast_to(token[g * group : (g + 1) * group], (group, META))
        column = jnp.concatenate([column, jnp.full((META - group, META), -1.0, F32)], axis=0)
        ac[c, z, slots : slots + 16, g * META : (g + 1) * META] = column.T[:16].astype(BF16)

    loads[2].wait()
    loads[3].wait()

    def turned(v):
        pieces = [
            v[(yy * RING + xx) * CAP : (yy * RING + xx + 1) * CAP]
            for xx in range(RING)
            for yy in range(RING)
        ]
        return jnp.concatenate(pieces, axis=0)

    @pl.loop(0, wg.shape[1] // tile)
    def _(j):
        cols = pl.ds(pl.multiple_of(j * tile, tile), tile)
        one = rh[0, :, :, :half].reshape(slots, half)
        two = rh[1, :, :, :half].reshape(slots, half)
        g = dot(one, wg[:half, cols]) + turned(dot(two, wg[half:, cols]))
        u = dot(one, wu[:half, cols]) + turned(dot(two, wu[half:, cols]))
        ac[c, z, :slots, cols] = (g / (1.0 + jnp.exp(-g)) * u * factor).astype(BF16)

    arow = ac.shape[2] // 32 * 16
    gg = Gather(
        lambda q: ac.at[c, q],
        lambda q: ac.at[c, q, pl.ds(0, arow)],
        lambda q: ac.at[c, q, pl.ds(arow, ac.shape[2] - arow)],
        z,
        z_plus,
        z_minus,
        gsend,
        grecv,
        sib,
    )
    gg.start()
    gg.pass_on()
    oo[:, group:META] = jnp.zeros((RING, META - group, oo.shape[2]), BF16)
    oo[:, META + group :] = jnp.zeros((RING, META - group, oo.shape[2]), BF16)
    loads[5].wait()
    gg.finish()
    gg.shared(lambda q: ac.at[d, q])

    width = oo.shape[2]
    deep = ac.shape[3]
    for e in range(2):
        for lo in range(0, width, tile):
            hi = min(lo + tile, width)
            res = jnp.zeros((slots, hi - lo), F32)
            for zz in range(2):
                for cc in range(2):
                    k = zz * 2 + cc
                    res += dot(ac[cc, e * 2 + zz, :slots, :], wd[e, k * deep : (k + 1) * deep, lo:hi])
            for g in range(RING):
                oo[g, e * META : e * META + group, lo:hi] = res[
                    g * group : (g + 1) * group
                ].astype(BF16)
    row_no = lax.broadcasted_iota(jnp.int32, (tokens, META), 0).astype(F32)
    ht = block // 2
    for g in range(RING):
        spread = [
            jnp.where(
                ac[0, e * 2, slots : slots + 1, g * META : (g + 1) * META].astype(F32) == row_no,
                1.0,
                0.0,
            ).astype(BF16)
            for e in range(2)
        ]
        sums = dot(jnp.concatenate(spread, axis=1), oo[g]).astype(BF16)
        for q in range(RING):
            pp[0, g, q] = sums[q * block : q * block + ht]
            pp[1, q, g] = sums[q * block + ht : (q + 1) * block]

    def scatter_sum(h, held, near, full, pos, plus, minus, base):
        before, after = dn1(pos), up1(pos)
        far = up1(after)
        depth = held.shape[1] // 2
        front, back = pl.ds(0, depth), pl.ds(depth, depth)
        one = remote(held.at[far, front], near.at[0], rsend.at[base], rrecv.at[base], plus)
        two = remote(held.at[far, back], near.at[1], rsend.at[base + 1], rrecv.at[base + 1], minus)
        three = remote(held.at[after], full.at[0], rsend.at[base + 2], rrecv.at[base + 2], plus)
        four = remote(held.at[before], full.at[1], rsend.at[base + 3], rrecv.at[base + 3], minus)

        def first():
            one.start()
            two.start()

        def second():
            one.wait_recv()
            held[after, :depth] = (held[after, :depth].astype(F32) + near[0].astype(F32)).astype(BF16)
            three.start()
            two.wait_recv()
            held[before, depth:] = (
                held[before, depth:].astype(F32) + near[1].astype(F32)
            ).astype(BF16)
            four.start()

        def third():
            three.wait_recv()
            four.wait_recv()
            for copy in (one, two, three, four):
                copy.wait_send()
            return held[pos].astype(F32) + full[0].astype(F32) + full[1].astype(F32)

        return first, second, third

    axes = ((x, x_plus, x_minus), (y, y_plus, y_minus))
    steps = [
        scatter_sum(h, pp.at[h], r1.at[h], r2.at[h], *axes[h], 4 * h) for h in range(2)
    ]
    more = [
        scatter_sum(h, t1.at[h], r3.at[h], r4.at[h], *axes[1 - h], 8 + 4 * h) for h in range(2)
    ]
    for first, _, _ in steps:
        first()
    for _, second, _ in steps:
        second()
    for h in range(2):
        t1[h] = steps[h][2]().astype(BF16)
        more[h][0]()
    for _, second, _ in more:
        second()
    cols = pl.ds(pl.multiple_of(lax.rem(local, RING) * width, 128), width)
    left = zh[z // 2, :, :, cols].reshape(block, width).astype(F32)
    for h in range(2):
        kept = pl.ds(h * ht, ht)
        out[h * ht : (h + 1) * ht] = (
            left[h * ht : (h + 1) * ht] + sres[kept, :] + more[h][2]()
        ).astype(BF16)

    for gather in (zg, ag, sh, gg):
        gather.drain()
    for copy in routed:
        copy.wait_send()


def body(hid, ids, aff, gain, gate, up, down, sgate, sup, sdown):
    rows, width = hid.shape
    half = width // 2
    block = rows * 2 * RING
    units = gate.shape[2]
    cols = down.shape[2]
    shared = sgate.shape[1]
    group = RING * CAP
    slots = RING * group
    ht = block // 2
    dma = pltpu.SemaphoreType.DMA
    hbm = pl.BlockSpec(memory_space=pl.ANY)
    vmem = pl.BlockSpec(memory_space=pltpu.VMEM)
    return pl.pallas_call(
        kernel,
        out_shape=jax.ShapeDtypeStruct((block, cols), BF16),
        in_specs=[vmem] * 4 + [hbm] * 6,
        out_specs=vmem,
        scratch_shapes=[
            pltpu.VMEM((width, units), BF16),
            pltpu.VMEM((width, units), BF16),
            pltpu.VMEM(down.shape, BF16),
            pltpu.VMEM(sgate.shape, BF16),
            pltpu.VMEM(sup.shape, BF16),
            pltpu.VMEM(sdown.shape, BF16),
            pltpu.VMEM((rows, half + META), F32),
            pltpu.VMEM((rows, half + META), F32),
            pltpu.VMEM((2, RING, 2 * rows, half + META), BF16),
            pltpu.VMEM((RING, block, half + META), BF16),
            pltpu.VMEM((block, half), BF16),
            pltpu.VMEM((META, RING * block), F32),
            pltpu.VMEM((3, group, half + META), BF16),
            pltpu.VMEM((2, group // 2, half + META), BF16),
            pltpu.VMEM((2, RING, group, half + META), BF16),
            pltpu.VMEM((2, RING, slots + 16, units), BF16),
            pltpu.VMEM((2, RING, block, shared), BF16),
            pltpu.VMEM((block, cols), F32),
            pltpu.VMEM((RING, 2 * META, cols), BF16),
            pltpu.VMEM((2, RING, RING, ht, cols), BF16),
            pltpu.VMEM((2, 2, RING // 2, ht, cols), BF16),
            pltpu.VMEM((2, 2, RING, ht, cols), BF16),
            pltpu.VMEM((2, RING, ht, cols), BF16),
            pltpu.VMEM((2, 2, ht // 2, cols), BF16),
            pltpu.VMEM((2, 2, ht, cols), BF16),
            dma((6,)),
            dma((2,)),
            dma((8,)),
            dma((8,)),
            dma((4,)),
            dma((4,)),
            dma((8,)),
            dma((8,)),
            dma((10,)),
            dma((10,)),
            dma((8,)),
            dma((8,)),
            dma((16,)),
            dma((16,)),
        ],
        compiler_params=pltpu.CompilerParams(
            collective_id=0, has_side_effects=True, vmem_limit_bytes=63 * 1024 * 1024
        ),
    )(hid, ids, aff, gain.reshape(2, 1, half), gate, up, down, sgate, sup, sdown)


def solution(mesh):
    in_specs = (
        P(("node", "local"), None),
        P(("node", "local"), None),
        P(("node", "local"), None),
        P(),
        P(("node", "local"), None, None),
        P(("node", "local"), None, None),
        P("node", None, "local"),
        P(None, "local"),
        P(None, "local"),
        P(None, "local"),
    )
    return jax.shard_map(
        body, mesh=mesh, in_specs=in_specs, out_specs=P("node", "local"), check_vma=False
    )
```

time: 344 us -> 105 us (0.31)
  waiting for transfers between devices: 194 us -> 0 us
  Pallas kernels: 0 us -> 103 us
  blocking collectives: 51.8 us -> 0 us
  local copies, waits for them, and re-layouts: 35.5 us -> 1.55 us
  matrix products: 25.7 us -> 0 us
  starting transfers between devices: 17.3 us -> 0 us
  between operations: 13.6 us -> 0.01 us
  other arithmetic: 4.21 us -> 0 us
    all_to_all x3 -> x0, waiting for transfers between devices: 169 us -> none  [the longest x1 166 us: body(): lax.all_to_all(buffer, 'node', split_axis=0, concat_axis=2, tiled=True)]
    pallas_call x0 -> x1, Pallas kernels: none -> 103 us  [body(): pl.pallas_call(kernel, out_shape=jax.ShapeDtypeStruct((block, cols), BF16...]
    all_gather x4 -> x0, blocking collectives: 51.8 us -> none  [the longest x1 14.2 us: body(): node_ids = lax.all_gather(expert_ids, 'local', axis=0, tiled=True)]
    dot_general x6 -> x0, matrix products: 25.7 us -> none  [the longest x1 7.45 us: body(): jnp.einsum('rep,epd->erd', act_all, down_w, preferred_element_type=jnp.fl...]
    all_gather x1 -> x0, waiting for transfers between devices: 25.7 us -> none  [body(): lax.all_gather(act, 'local', axis=1, tiled=True)]
    scatter x1 -> x0, local copies, waits for them, and re-layouts: 18.7 us -> none  [body(): jnp.zeros((expert_count * capacity, width), jnp.bfloat16).at[target]]
    all_to_all x3 -> x0, starting transfers between devices: 17.3 us -> none  [the longest x1 7.08 us: body(): lax.all_to_all(buffer, 'node', split_axis=0, concat_axis=2, tiled=True)]
    gather x2 -> x0, local copies, waits for them, and re-layouts: 9.06 us -> none  [the longest x1 7 us: body(): spread_rows = node_rows[row_of]]
  transfers between devices with their start and end apart: 4 -> 0, of which waited for: 3 -> 0; matrix products, arithmetic and copies ran while one was open for 2% -> 0% of each run, Pallas kernels for 0% -> 0%
where the time goes in v1:
time: 105 us
  Pallas kernels  103 us (98%)
  local copies, waits for them, and re-layouts  1.55 us (1%)
    pallas_call x1, Pallas kernels, body(): pl.pallas_call(kernel, out_shape=jax.ShapeDtypeStruct((block, cols), BF16...  103 us

profile of v1, /device:TPU:0, one launch (start us, length us, event | category | flops | bytes accessed | tf_op | source)
XLA Modules:
  0.0 104.5 jit_solution(8066513685593862139)
XLA Ops:
  0.0 103.0 %shard_map.100 = bf16[64,896]{1,0:T(8,128)(2,1)} custom-call(bf16[8,7168]{1,0:T(8,128)(2,1)} %hid.1, s32[8,8]{1,0:T(8,128)} %ids.1, bf16[8,8]{1,0:T(8,128)(2,1)} %aff.1, f32[2,1,3584]{2,1,0:T(1,128)} %bitcast.1, bf16[1,7168,512]{2,1,0:T(8,128)(2,1)} %gate_hbm.1, bf16[1,7168,512]{2,1,0:T(8,128)(2,1)} %up_hbm.1, bf16[2,2048,896]{2,1,0:T(8,128)(2,1)} %down_hbm.1, ...), custom_call_target="tpu_custom_call" | custom-call | tf_op jit(solution)/shard_map/pallas_call | solution.py:529
  103.0 1.6 %copy.12 = bf16[64,896]{1,0:T(8,128)(2,1)} copy(bf16[64,896]{1,0:T(8,128)(2,1)} %shard_map.100) | data formatting | bytes 229376

commit v2 on v1

v2 whole, which is shorter than its diff:
```python
import functools

import jax
import jax.numpy as jnp
from jax import lax
from jax.experimental import pallas as pl
from jax.experimental.pallas import tpu as pltpu
from jax.sharding import PartitionSpec as P

MESH = pl.DeviceIdType.MESH
F32 = jnp.float32
BF16 = jnp.bfloat16
RING = 4
META = 128
CAP = 24
TOP = 8


def remote(src, dst, send, recv, device):
    return pltpu.make_async_remote_copy(
        src_ref=src,
        dst_ref=dst,
        send_sem=send,
        recv_sem=recv,
        device_id=device,
        device_id_type=MESH,
    )


def dot(a, b):
    return jnp.dot(a, b, preferred_element_type=F32)


class Gather:
    def __init__(self, slot, pos, peers, send, recv, other):
        self.slot, self.pos, self.peers, self.other = slot, pos, peers, other
        self.send, self.recv = send, recv
        self.origins = [lax.rem(pos + step, RING) for step in (3, 1, 2)]
        self.sent = []

    def copy(self, ref, index, device):
        return remote(ref, ref, self.send.at[index], self.recv.at[index], device)

    def go(self, ref, index, device):
        copy = self.copy(ref, index, device)
        copy.start()
        self.sent.append(copy)

    def start(self):
        for index, device in enumerate(self.peers):
            self.go(self.slot(self.pos), index, device)
        self.go(self.slot(self.pos), 3, self.other)

    def arrive(self):
        for index, origin in enumerate(self.origins):
            self.copy(self.slot(origin), index, self.other).wait_recv()
            self.go(self.slot(origin), 4 + index, self.other)

    def shared(self, mirror):
        for index, origin in enumerate([self.pos] + self.origins):
            self.copy(mirror(origin), 3 + index, self.other).wait_recv()

    def drain(self):
        for copy in self.sent:
            copy.wait_send()


def kernel(
    hid,
    ids,
    aff,
    gain,
    gate_hbm,
    up_hbm,
    down_hbm,
    sgate_hbm,
    sup_hbm,
    sdown_hbm,
    out,
    wg,
    wu,
    wd,
    sg,
    su,
    sd,
    pair_out,
    pair_in,
    zh,
    xa,
    xo,
    ct,
    pm,
    cs,
    rh,
    ac,
    sa,
    sres,
    oo,
    pp,
    r1,
    r2,
    t1,
    wsem,
    bsem,
    zsend,
    zrecv,
    asend,
    arecv,
    ssend,
    srecv,
    csend,
    crecv,
    gsend,
    grecv,
    rsend,
    rrecv,
):
    half = hid.shape[1] // 2
    node, local = lax.axis_index("node"), lax.axis_index("local")
    y, x = node // RING, lax.rem(node, RING)
    z, c = local // 2, lax.rem(local, 2)
    d = 1 - c
    sib = (node, z * 2 + d)
    moves = (1, 3, 2)
    step = lambda v, by: lax.rem(v + by, RING)
    z_peers = [(node, step(z, by) * 2 + c) for by in moves]
    x_peers = [(y * RING + step(x, by), local) for by in moves]
    y_peers = [(step(y, by) * RING + x, local) for by in moves]
    a_peers = [(d * v[0] + c * u[0], local) for u, v in zip(x_peers, y_peers)]
    b_peers = [(d * u[0] + c * v[0], local) for u, v in zip(x_peers, y_peers)]
    apos, bpos = d * y + c * x, d * x + c * y

    barrier = pltpu.get_barrier_semaphore()
    everyone = [sib] + z_peers + x_peers + y_peers
    for peer in everyone:
        pl.semaphore_signal(barrier, inc=1, device_id=peer, device_id_type=MESH)

    values = hid[...].astype(F32)
    scale = lax.rsqrt(jnp.mean(values * values, axis=-1, keepdims=True) + 1e-06)
    s_hi = scale.astype(BF16).astype(F32)
    s_mid = (scale - s_hi).astype(BF16).astype(F32)
    s_lo = scale - s_hi - s_mid
    weight = aff[...].astype(F32)
    mix = 2.5 * weight / jnp.sum(weight, axis=-1, keepdims=True)
    m_hi = mix.astype(BF16).astype(F32)
    m_lo = mix - m_hi
    named = ids[...].astype(F32)
    rows = hid.shape[0]
    lane = lax.broadcasted_iota(jnp.int32, (rows, META), 1)
    place = (z * 2 * rows + c * rows + lax.broadcasted_iota(jnp.int32, (rows, META), 0)).astype(F32)
    meta = jnp.where(lane == 16, place, 0.0)
    meta = jnp.where(lane == 17, 1.0, meta)
    meta = jnp.where(lane == 18, s_hi, meta)
    meta = jnp.where(lane == 19, s_mid, meta)
    meta = jnp.where(lane == 20, s_lo, meta)
    for k in range(TOP):
        meta = jnp.where(lane == k, named[:, k : k + 1], meta)
        meta = jnp.where(lane == 8 + k, m_hi[:, k : k + 1], meta)
        meta = jnp.where(lane == 24 + k, m_lo[:, k : k + 1], meta)
    other_cols = pl.ds(pl.multiple_of(d * half, 128), half)
    own_cols = pl.ds(pl.multiple_of(c * half, 128), half)
    pair_out[:, :half] = hid[:, other_cols].astype(F32)
    pair_out[:, half:] = meta

    pl.semaphore_wait(barrier, len(everyone))
    pair = remote(pair_out, pair_in, bsem.at[0], bsem.at[1], sib)
    pair.start()
    loads = [
        pltpu.make_async_copy(src, dst, wsem.at[i])
        for i, (src, dst) in enumerate(
            (
                (sgate_hbm, sg),
                (sup_hbm, su),
                (gate_hbm.at[0], wg),
                (up_hbm.at[0], wu),
                (sdown_hbm, sd),
                (down_hbm, wd),
            )
        )
    ]
    for load in loads:
        load.start()
    own = jnp.concatenate([hid[:, own_cols].astype(F32), meta], axis=1)
    pair.wait()
    theirs = pair_in[...]
    zh[c, z] = jnp.concatenate(
        [jnp.where(c == 0, own, theirs), jnp.where(c == 0, theirs, own)], axis=0
    ).astype(BF16)

    zg = Gather(lambda q: zh.at[c, q], z, z_peers, zsend, zrecv, sib)
    zg.start()
    zg.arrive()

    block = RING * zh.shape[2]

    def normed(h):
        held = zh[h].reshape(block, half + META)
        info = held[:, half:].astype(F32)
        by = info[:, 18:19] + info[:, 19:20] + info[:, 20:21]
        return (held[:, :half].astype(F32) * by * gain[h]).astype(BF16)

    xa[apos, :, :half] = normed(c)
    xa[apos, :, half:] = zh[c, :, :, half:].reshape(block, META)

    part = block // 2
    upper, lower = pl.ds(0, part), pl.ds(part, part)
    a_prev, a_next, a_far = step(apos, 3), step(apos, 1), step(apos, 2)

    def ring(place, rows, index, device):
        return remote(
            xa.at[place, rows], xa.at[place, rows], asend.at[index], arecv.at[index], device
        )

    around = [
        ring(apos, upper, 0, a_peers[0]),
        ring(apos, lower, 1, a_peers[1]),
        ring(apos, lower, 2, a_peers[0]),
        ring(apos, upper, 3, a_peers[1]),
    ]
    for copy in around:
        copy.start()
    zg.shared(lambda q: zh.at[d, q])
    xo[...] = normed(d)

    loads[0].wait()
    loads[1].wait()
    own_rows = pl.ds(pl.multiple_of(c * half, 128), half)
    other_rows = pl.ds(pl.multiple_of(d * half, 128), half)
    mine = xa[apos, :, :half]
    s_gate = dot(mine, sg[own_rows, :]) + dot(xo[...], sg[other_rows, :])
    s_up = dot(mine, su[own_rows, :]) + dot(xo[...], su[other_rows, :])
    sa[c, z] = (s_gate / (1.0 + jnp.exp(-s_gate)) * s_up).astype(BF16)
    ring(a_prev, upper, 0, a_peers[0]).wait_recv()
    around.append(ring(a_prev, upper, 4, a_peers[0]))
    around[4].start()
    ring(a_next, lower, 1, a_peers[1]).wait_recv()
    around.append(ring(a_next, lower, 5, a_peers[1]))
    around[5].start()
    sh = Gather(lambda q: sa.at[c, q], z, z_peers, ssend, srecv, sib)
    sh.start()
    ring(a_prev, lower, 2, a_peers[0]).wait_recv()
    ring(a_next, upper, 3, a_peers[1]).wait_recv()
    ring(a_far, upper, 4, a_peers[0]).wait_recv()
    ring(a_far, lower, 5, a_peers[1]).wait_recv()

    tokens = RING * block
    info = xa[:, :, half:].reshape(tokens, META).astype(F32)
    lane = lax.broadcasted_iota(jnp.int32, (tokens, META), 1).astype(F32)
    names = jnp.zeros((tokens, META), F32)
    for k in range(TOP):
        names = jnp.where(info[:, k : k + 1] == lane, 1.0, names)
    t_row = lax.broadcasted_iota(jnp.int32, (tokens, tokens), 0)
    t_col = lax.broadcasted_iota(jnp.int32, (tokens, tokens), 1)
    earlier = jnp.where((t_col < t_row) & (t_col // block == t_row // block), 1.0, 0.0)
    counts = dot(earlier.astype(BF16), names.astype(BF16))
    base = (lax.broadcasted_iota(jnp.int32, (tokens, META), 0) // (2 * block) * CAP).astype(F32)
    ct[...] = jnp.where(names > 0.5, counts + base, -1.0).T

    duo = 2 * CAP
    tile = 256
    tiles = half // tile
    slot_no = lax.broadcasted_iota(jnp.int32, (duo, tokens), 0).astype(F32)
    parity = lax.rem(lax.broadcasted_iota(jnp.int32, (duo, tokens), 1) // block, 2)
    routed = []

    def pick(group):
        chosen = []
        for by in range(RING):
            there = step(bpos, by)
            expert = (d * (y * RING + there) + c * (there * RING + x)) * 2 + z // 2
            hit = (ct[pl.ds(expert, 1), :] == slot_no) & (parity == lax.rem(bpos + group, 2))
            chosen.append(jnp.where(hit, 1.0, 0.0).astype(BF16))
        pm[...] = jnp.concatenate(chosen, axis=0)

        def put(cols, picked):
            rh[c, group, bpos, :, cols] = picked[:duo]
            for i in range(3):
                cs[group, i, :, cols] = picked[(i + 1) * duo : (i + 2) * duo]

        @pl.loop(0, tiles)
        def _(j):
            cols = pl.ds(pl.multiple_of(j * tile, tile), tile)
            put(cols, dot(pm[...], xa[:, :, cols].reshape(tokens, tile)).astype(BF16))

        put(
            pl.ds(half, META),
            dot(pm[...], xa[:, :, half:].reshape(tokens, META)).astype(BF16),
        )
        for index in (2, 0, 1):
            send(group, index).start()
        give(group, bpos, 0)

    def send(group, index):
        sem = group * 3 + index
        copy = remote(
            cs.at[group, moves[index] - 1],
            rh.at[c, group, bpos],
            csend.at[sem],
            crecv.at[sem],
            b_peers[index],
        )
        routed.append(copy)
        return copy

    def give(group, place, index):
        sem = 6 + group * 4 + index
        ref = rh.at[c, group, place]
        copy = remote(ref, ref, csend.at[sem], crecv.at[sem], sib)
        copy.start()
        routed.append(copy)

    pick(0)
    pick(1)
    sh.arrive()
    sh.shared(lambda q: sa.at[d, q])
    loads[4].wait()
    total = jnp.zeros(sres.shape, F32)
    wide = sa.shape[3]
    for zz in range(RING):
        for cc in range(2):
            total += dot(sa[cc, zz], sd[(zz * 2 + cc) * wide : (zz * 2 + cc + 1) * wide, :])
    sres[...] = total
    oo[:, :, 2 * duo : META] = jnp.zeros((2, 2, META - 2 * duo, oo.shape[3]), BF16)
    oo[:, :, META + 2 * duo :] = jnp.zeros((2, 2, META - 2 * duo, oo.shape[3]), BF16)

    def collect(group):
        for index, by in ((0, 3), (1, 1), (2, 2)):
            sem = group * 3 + index
            place = step(bpos, by)
            remote(
                cs.at[group, 0], rh.at[c, group, place], csend.at[sem], crecv.at[sem], sib
            ).wait_recv()
            give(group, place, index + 1)
        for index, by in ((0, 0), (1, 3), (2, 1), (3, 2)):
            sem = 6 + group * 4 + index
            ref = rh.at[d, group, step(apos, by)]
            remote(ref, ref, csend.at[sem], crecv.at[sem], sib).wait_recv()

    slots = RING * duo
    expert = (node * 2 + z // 2).astype(F32)

    def turned(v, group):
        pieces = []
        for xx in range(RING):
            for k in range(2):
                at = (2 * k + (xx + group) % 2) * 2 + xx // 2
                pieces.append(v[at * CAP : (at + 1) * CAP])
        return jnp.concatenate(pieces, axis=0)

    def hidden(group):
        info = rh[0, group, :, :, half:].reshape(slots, META).astype(F32)
        lane = lax.broadcasted_iota(jnp.int32, (slots, META), 1)
        shares = pltpu.roll(info, META - 8, 1) + pltpu.roll(info, META - 24, 1)
        factor = jnp.sum(
            jnp.where((lane < TOP) & (info == expert), shares, 0.0), axis=1, keepdims=True
        )
        s_no = lax.broadcasted_iota(jnp.int32, (slots, 1), 0)
        home = (lax.rem(s_no // CAP, RING) * block).astype(F32)
        token = jnp.where(info[:, 17:18] > 0.5, info[:, 16:17] + home, -1.0)
        for i in range(2):
            column = jnp.broadcast_to(token[i * 2 * duo : (i + 1) * 2 * duo], (2 * duo, META))
            column = jnp.concatenate(
                [column, jnp.full((META - 2 * duo, META), -1.0, F32)], axis=0
            )
            ac[c, z, group, slots:, i * META : (i + 1) * META] = column.T[:16].astype(BF16)
        ac[c, z, group, slots:, 2 * META :] = jnp.zeros((16, ac.shape[4] - 2 * META), BF16)

        @pl.loop(0, wg.shape[1] // tile)
        def _(j):
            cols = pl.ds(pl.multiple_of(j * tile, tile), tile)
            one = rh[0, group, :, :, :half].reshape(slots, half)
            two = rh[1, group, :, :, :half].reshape(slots, half)
            g = dot(one, wg[:half, cols]) + turned(dot(two, wg[half:, cols]), group)
            u = dot(one, wu[:half, cols]) + turned(dot(two, wu[half:, cols]), group)
            ac[c, z, group, :slots, cols] = (g / (1.0 + jnp.exp(-g)) * u * factor).astype(BF16)

        return Gather(
            lambda q: ac.at[c, q, group], z, z_peers, gsend.at[group], grecv.at[group], sib
        )

    collect(0)
    loads[2].wait()
    loads[3].wait()
    gg = [hidden(0)]
    gg[0].start()
    collect(1)
    gg.append(hidden(1))
    gg[1].start()

    width = oo.shape[3]
    deep = ac.shape[4]
    ht = block // 2
    row_no = lax.broadcasted_iota(jnp.int32, (tokens, META), 0).astype(F32)

    def outputs(group):
        for e in range(2):
            for lo in range(0, width, tile):
                hi = min(lo + tile, width)
                res = jnp.zeros((slots, hi - lo), F32)
                for zz in range(2):
                    for cc in range(2):
                        k = zz * 2 + cc
                        res += dot(
                            ac[cc, e * 2 + zz, group, :slots, :],
                            wd[e, k * deep : (k + 1) * deep, lo:hi],
                        )
                for i in range(2):
                    oo[group, i, e * META : e * META + 2 * duo, lo:hi] = res[
                        i * 2 * duo : (i + 1) * 2 * duo
                    ].astype(BF16)
        for i in range(2):
            spread = [
                jnp.where(
                    ac[0, e * 2, group, slots : slots + 1, i * META : (i + 1) * META].astype(F32)
                    == row_no,
                    1.0,
                    0.0,
                ).astype(BF16)
                for e in range(2)
            ]
            sums = dot(jnp.concatenate(spread, axis=1), oo[group, i]).astype(BF16)
            for p in range(2):
                for k in range(2):
                    xx = i * 2 + p
                    yy = 2 * k + (xx + group) % 2
                    at = (p * 2 + k) * block
                    pp[0, group, xx, k] = sums[at : at + ht]
                    pp[1, group, yy, i] = sums[at + ht : at + block]

    axes = ((x, x_peers), (y, y_peers))
    sums1, sums2 = [], []

    def spread_first(group):
        for h in range(2):
            pos, peers = axes[h]
            for index, by in enumerate(moves):
                sem = (group * 2 + h) * 3 + index
                copy = remote(
                    pp.at[h, group, step(pos, by)],
                    r1.at[h, group, index],
                    rsend.at[sem],
                    rrecv.at[sem],
                    peers[index],
                )
                copy.start()
                sums1.append(copy)

    def sum_first(group):
        for h in range(2):
            pos = axes[h][0]
            for index in range(3):
                sums1[(group * 2 + h) * 3 + index].wait_recv()
            whole = pp[h, group, pos].astype(F32)
            for index in range(3):
                whole += r1[h, group, index].astype(F32)
            for k in range(2):
                t1[h, 2 * k + lax.rem(pos + group, 2)] = whole[k].astype(BF16)

    gg[0].arrive()
    gg[0].shared(lambda q: ac.at[d, q, 0])
    loads[5].wait()
    outputs(0)
    spread_first(0)
    gg[1].arrive()
    gg[1].shared(lambda q: ac.at[d, q, 1])
    outputs(1)
    spread_first(1)
    sum_first(0)
    sum_first(1)
    for h in range(2):
        pos, peers = axes[1 - h]
        for index, by in enumerate(moves):
            sem = 12 + h * 3 + index
            copy = remote(
                t1.at[h, step(pos, by)],
                r2.at[h, index],
                rsend.at[sem],
                rrecv.at[sem],
                peers[index],
            )
            copy.start()
            sums2.append(copy)
    cols = pl.ds(pl.multiple_of(lax.rem(local, RING) * width, 128), width)
    left = zh[z // 2, :, :, cols].reshape(block, width).astype(F32) + sres[...]
    for h in range(2):
        pos = axes[1 - h][0]
        whole = left[h * ht : (h + 1) * ht] + t1[h, pos].astype(F32)
        for index in range(3):
            sums2[h * 3 + index].wait_recv()
            whole += r2[h, index].astype(F32)
        out[h * ht : (h + 1) * ht] = whole.astype(BF16)

    for gather in [zg, sh] + gg:
        gather.drain()
    for copy in around + routed + sums1 + sums2:
        copy.wait_send()


def body(hid, ids, aff, gain, gate, up, down, sgate, sup, sdown):
    rows, width = hid.shape
    half = width // 2
    block = rows * 2 * RING
    units = gate.shape[2]
    cols = down.shape[2]
    shared = sgate.shape[1]
    duo = 2 * CAP
    slots = RING * duo
    ht = block // 2
    dma = pltpu.SemaphoreType.DMA
    hbm = pl.BlockSpec(memory_space=pl.ANY)
    vmem = pl.BlockSpec(memory_space=pltpu.VMEM)
    return pl.pallas_call(
        kernel,
        out_shape=jax.ShapeDtypeStruct((block, cols), BF16),
        in_specs=[vmem] * 4 + [hbm] * 6,
        out_specs=vmem,
        scratch_shapes=[
            pltpu.VMEM((width, units), BF16),
            pltpu.VMEM((width, units), BF16),
            pltpu.VMEM(down.shape, BF16),
            pltpu.VMEM(sgate.shape, BF16),
            pltpu.VMEM(sup.shape, BF16),
            pltpu.VMEM(sdown.shape, BF16),
            pltpu.VMEM((rows, half + META), F32),
            pltpu.VMEM((rows, half + META), F32),
            pltpu.VMEM((2, RING, 2 * rows, half + META), BF16),
            pltpu.VMEM((RING, block, half + META), BF16),
            pltpu.VMEM((block, half), BF16),
            pltpu.VMEM((META, RING * block), F32),
            pltpu.VMEM((slots, RING * block), BF16),
            pltpu.VMEM((2, 3, duo, half + META), BF16),
            pltpu.VMEM((2, 2, RING, duo, half + META), BF16),
            pltpu.VMEM((2, RING, 2, slots + 16, units), BF16),
            pltpu.VMEM((2, RING, block, shared), BF16),
            pltpu.VMEM((block, cols), F32),
            pltpu.VMEM((2, 2, 2 * META, cols), BF16),
            pltpu.VMEM((2, 2, RING, 2, ht, cols), BF16),
            pltpu.VMEM((2, 2, 3, 2, ht, cols), BF16),
            pltpu.VMEM((2, 3, ht, cols), BF16),
            pltpu.VMEM((2, RING, ht, cols), BF16),
            dma((6,)),
            dma((2,)),
            dma((7,)),
            dma((7,)),
            dma((6,)),
            dma((6,)),
            dma((7,)),
            dma((7,)),
            dma((14,)),
            dma((14,)),
            dma((2, 7)),
            dma((2, 7)),
            dma((18,)),
            dma((18,)),
        ],
        compiler_params=pltpu.CompilerParams(
            collective_id=0, has_side_effects=True, vmem_limit_bytes=63 * 1024 * 1024
        ),
    )(hid, ids, aff, gain.reshape(2, 1, half), gate, up, down, sgate, sup, sdown)


def solution(mesh):
    in_specs = (
        P(("node", "local"), None),
        P(("node", "local"), None),
        P(("node", "local"), None),
        P(),
        P(("node", "local"), None, None),
        P(("node", "local"), None, None),
        P("node", None, "local"),
        P(None, "local"),
        P(None, "local"),
        P(None, "local"),
    )
    return jax.shard_map(
        body, mesh=mesh, in_specs=in_specs, out_specs=P("node", "local"), check_vma=False
    )
```

time: 105 us -> 86.3 us (0.82)
  Pallas kernels: 103 us -> 84.6 us
    pallas_call x1, Pallas kernels: 103 us -> 84.6 us  [body(): pl.pallas_call(kernel, out_shape=jax.ShapeDtypeStruct((block, cols), BF16...]
where the time goes in v2:
time: 86.3 us; the launch traced here: 86.1 us
  Pallas kernels  84.6 us (98%)
  local copies, waits for them, and re-layouts  1.55 us (2%)
    pallas_call x1, Pallas kernels, body(): pl.pallas_call(kernel, out_shape=jax.ShapeDtypeStruct((block, cols), BF16...  84.6 us

profile of v2, /device:TPU:0, one launch (start us, length us, event | category | flops | bytes accessed | tf_op | source)
XLA Modules:
  0.0 86.1 jit_solution(14250635560843861594)
XLA Ops:
  0.0 84.6 %shard_map.100 = bf16[64,896]{1,0:T(8,128)(2,1)} custom-call(bf16[8,7168]{1,0:T(8,128)(2,1)} %hid.1, s32[8,8]{1,0:T(8,128)} %ids.1, bf16[8,8]{1,0:T(8,128)(2,1)} %aff.1, f32[2,1,3584]{2,1,0:T(1,128)} %bitcast.1, bf16[1,7168,512]{2,1,0:T(8,128)(2,1)} %gate_hbm.1, bf16[1,7168,512]{2,1,0:T(8,128)(2,1)} %up_hbm.1, bf16[2,2048,896]{2,1,0:T(8,128)(2,1)} %down_hbm.1, ...), custom_call_target="tpu_custom_call" | custom-call | tf_op jit(solution)/shard_map/pallas_call | solution.py:512
  84.6 1.6 %copy.12 = bf16[64,896]{1,0:T(8,128)(2,1)} copy(bf16[64,896]{1,0:T(8,128)(2,1)} %shard_map.100) | data formatting | bytes 229376

commit v3 on v2

--- a/solution.py
+++ b/solution.py
@@ -83,9 +83,10 @@
     sg,
     su,
     sd,
-    pair_out,
-    pair_in,
-    zh,
+    pa,
+    pb,
+    za,
+    zb,
     xa,
     xo,
     ct,
@@ -101,7 +102,6 @@
     r2,
     t1,
     wsem,
-    bsem,
     zsend,
     zrecv,
     asend,
@@ -126,12 +126,13 @@
     z_peers = [(node, step(z, by) * 2 + c) for by in moves]
     x_peers = [(y * RING + step(x, by), local) for by in moves]
     y_peers = [(step(y, by) * RING + x, local) for by in moves]
+    z_cross = [(node, step(z, by) * 2 + d) for by in moves]
     a_peers = [(d * v[0] + c * u[0], local) for u, v in zip(x_peers, y_peers)]
     b_peers = [(d * u[0] + c * v[0], local) for u, v in zip(x_peers, y_peers)]
     apos, bpos = d * y + c * x, d * x + c * y
 
     barrier = pltpu.get_barrier_semaphore()
-    everyone = [sib] + z_peers + x_peers + y_peers
+    everyone = [sib] + z_peers + z_cross + x_peers + y_peers
     for peer in everyone:
         pl.semaphore_signal(barrier, inc=1, device_id=peer, device_id_type=MESH)
 
@@ -157,14 +158,35 @@
         meta = jnp.where(lane == k, named[:, k : k + 1], meta)
         meta = jnp.where(lane == 8 + k, m_hi[:, k : k + 1], meta)
         meta = jnp.where(lane == 24 + k, m_lo[:, k : k + 1], meta)
-    other_cols = pl.ds(pl.multiple_of(d * half, 128), half)
-    own_cols = pl.ds(pl.multiple_of(c * half, 128), half)
-    pair_out[:, :half] = hid[:, other_cols].astype(F32)
-    pair_out[:, half:] = meta
-
+    quarter = half // 2
+    eighth = quarter // 2
+
+    def laid(h, start):
+        cols = lambda i: pl.ds(pl.multiple_of(h * half + start + i * eighth, 128), eighth)
+        return jnp.concatenate([hid[:, cols(i)].astype(F32) for i in range(2)], axis=0)
+
+    beside = jnp.concatenate([meta, jnp.zeros((rows, META), F32)], axis=0).astype(BF16)
+    za[c, local, :, :eighth] = laid(c, quarter).astype(BF16)
+    za[c, local, :, eighth:] = beside
+    zb[c, local] = laid(c, 0).astype(BF16)
+    pa[:, :eighth] = laid(d, quarter).astype(BF16)
+    pa[:, eighth:] = beside
+    pb[...] = laid(d, 0).astype(BF16)
     pl.semaphore_wait(barrier, len(everyone))
-    pair = remote(pair_out, pair_in, bsem.at[0], bsem.at[1], sib)
-    pair.start()
+    first = []
+    for part, (mine, other, held) in enumerate(((za.at[c, local], pa, za), (zb.at[c, local], pb, zb))):
+        for index, device in enumerate(z_peers + z_cross + [sib]):
+            whose = c if index < 3 else d
+            sem = part * 7 + index
+            copy = remote(
+                mine if index < 3 else other,
+                held.at[whose, local],
+                zsend.at[sem],
+                zrecv.at[sem],
+                device,
+            )
+            copy.start()
+            first.append(copy)
     loads = [
         pltpu.make_async_copy(src, dst, wsem.at[i])
         for i, (src, dst) in enumerate(
@@ -180,68 +202,82 @@
     ]
     for load in loads:
         load.start()
-    own = jnp.concatenate([hid[:, own_cols].astype(F32), meta], axis=1)
-    pair.wait()
-    theirs = pair_in[...]
-    zh[c, z] = jnp.concatenate(
-        [jnp.where(c == 0, own, theirs), jnp.where(c == 0, theirs, own)], axis=0
-    ).astype(BF16)
-
-    zg = Gather(lambda q: zh.at[c, q], z, z_peers, zsend, zrecv, sib)
-    zg.start()
-    zg.arrive()
-
-    block = RING * zh.shape[2]
-
-    def normed(h):
-        held = zh[h].reshape(block, half + META)
-        info = held[:, half:].astype(F32)
+
+    def gathered(part):
+        held = (za, zb)[part]
+        back = (3, 1, 2)
+        origins = [step(z, by) * 2 + c for by in back] + [step(z, by) * 2 + d for by in back]
+        origins.append(z * 2 + d)
+        for index, origin in enumerate(origins):
+            sem = part * 7 + index
+            ref = held.at[c, origin]
+            remote(ref, ref, zsend.at[sem], zrecv.at[sem], sib).wait_recv()
+        copy = remote(held.at[c], held.at[c], zsend.at[14 + part], zrecv.at[14 + part], sib)
+        first.append(copy)
+        return copy
+
+    block = RING * 2 * rows
+    ahead = pl.ds(quarter, quarter + META)
+    behind = pl.ds(0, quarter)
+
+    def spread_out(held):
+        v = held.astype(F32).reshape(2 * RING, 2, rows, held.shape[2])
+        return [v[:, i].reshape(block, held.shape[2]) for i in range(2)]
+
+    def normed(h, part):
+        lead, rest = spread_out((za, zb)[part][h])
+        info = spread_out(za[h, :, :, eighth:])[0]
         by = info[:, 18:19] + info[:, 19:20] + info[:, 20:21]
-        return (held[:, :half].astype(F32) * by * gain[h]).astype(BF16)
-
-    xa[apos, :, :half] = normed(c)
-    xa[apos, :, half:] = zh[c, :, :, half:].reshape(block, META)
-
-    part = block // 2
-    upper, lower = pl.ds(0, part), pl.ds(part, part)
+        start = (quarter, 0)[part]
+        lead = lead[:, :eighth] * by * gain[h, :, start : start + eighth]
+        rest = rest[:, :eighth] * by * gain[h, :, start + eighth : start + quarter]
+        return jnp.concatenate([lead, rest], axis=1).astype(BF16)
+
+    part_rows = block // 2
+    upper, lower = pl.ds(0, part_rows), pl.ds(part_rows, part_rows)
     a_prev, a_next, a_far = step(apos, 3), step(apos, 1), step(apos, 2)
 
-    def ring(place, rows, index, device):
-        return remote(
-            xa.at[place, rows], xa.at[place, rows], asend.at[index], arecv.at[index], device
-        )
-
-    around = [
-        ring(apos, upper, 0, a_peers[0]),
-        ring(apos, lower, 1, a_peers[1]),
-        ring(apos, lower, 2, a_peers[0]),
-        ring(apos, upper, 3, a_peers[1]),
-    ]
-    for copy in around:
+    def ring(part, place, rows_of, index, device):
+        ref = xa.at[place, rows_of, (ahead, behind)[part]]
+        sem = part * 6 + index
+        return remote(ref, ref, asend.at[sem], arecv.at[sem], device)
+
+    around = []
+
+    def go(copy):
         copy.start()
-    zg.shared(lambda q: zh.at[d, q])
-    xo[...] = normed(d)
-
-    loads[0].wait()
-    loads[1].wait()
-    own_rows = pl.ds(pl.multiple_of(c * half, 128), half)
-    other_rows = pl.ds(pl.multiple_of(d * half, 128), half)
-    mine = xa[apos, :, :half]
-    s_gate = dot(mine, sg[own_rows, :]) + dot(xo[...], sg[other_rows, :])
-    s_up = dot(mine, su[own_rows, :]) + dot(xo[...], su[other_rows, :])
-    sa[c, z] = (s_gate / (1.0 + jnp.exp(-s_gate)) * s_up).astype(BF16)
-    ring(a_prev, upper, 0, a_peers[0]).wait_recv()
-    around.append(ring(a_prev, upper, 4, a_peers[0]))
-    around[4].start()
-    ring(a_next, lower, 1, a_peers[1]).wait_recv()
-    around.append(ring(a_next, lower, 5, a_peers[1]))
-    around[5].start()
-    sh = Gather(lambda q: sa.at[c, q], z, z_peers, ssend, srecv, sib)
-    sh.start()
-    ring(a_prev, lower, 2, a_peers[0]).wait_recv()
-    ring(a_next, upper, 3, a_peers[1]).wait_recv()
-    ring(a_far, upper, 4, a_peers[0]).wait_recv()
-    ring(a_far, lower, 5, a_peers[1]).wait_recv()
+        around.append(copy)
+
+    def ring_start(part):
+        go(ring(part, apos, upper, 0, a_peers[0]))
+        go(ring(part, apos, lower, 1, a_peers[1]))
+        go(ring(part, apos, lower, 2, a_peers[0]))
+        go(ring(part, apos, upper, 3, a_peers[1]))
+
+    def ring_on(part):
+        ring(part, a_prev, upper, 0, a_peers[0]).wait_recv()
+        go(ring(part, a_prev, upper, 4, a_peers[0]))
+        ring(part, a_next, lower, 1, a_peers[1]).wait_recv()
+        go(ring(part, a_next, lower, 5, a_peers[1]))
+
+    def ring_end(part):
+        ring(part, a_prev, lower, 2, a_peers[0]).wait_recv()
+        ring(part, a_next, upper, 3, a_peers[1]).wait_recv()
+        ring(part, a_far, upper, 4, a_peers[0]).wait_recv()
+        ring(part, a_far, lower, 5, a_peers[1]).wait_recv()
+
+    share = gathered(0)
+    xa[apos, :, quarter:half] = normed(c, 0)
+    xa[apos, :, half:] = spread_out(za[c, :, :, eighth:])[0].astype(BF16)
+    ring_start(0)
+    share.start()
+    share = gathered(1)
+    xa[apos, :, :quarter] = normed(c, 1)
+    ring_start(1)
+    share.start()
+    ring_on(0)
+    ring_on(1)
+    ring_end(0)
 
     tokens = RING * block
     info = xa[:, :, half:].reshape(tokens, META).astype(F32)
@@ -258,43 +294,41 @@
 
     duo = 2 * CAP
     tile = 256
-    tiles = half // tile
+    tiles = quarter // tile
     slot_no = lax.broadcasted_iota(jnp.int32, (duo, tokens), 0).astype(F32)
     parity = lax.rem(lax.broadcasted_iota(jnp.int32, (duo, tokens), 1) // block, 2)
     routed = []
 
-    def pick(group):
-        chosen = []
+    def choose(group):
         for by in range(RING):
             there = step(bpos, by)
             expert = (d * (y * RING + there) + c * (there * RING + x)) * 2 + z // 2
             hit = (ct[pl.ds(expert, 1), :] == slot_no) & (parity == lax.rem(bpos + group, 2))
-            chosen.append(jnp.where(hit, 1.0, 0.0).astype(BF16))
-        pm[...] = jnp.concatenate(chosen, axis=0)
-
-        def put(cols, picked):
+            pm[group, by * duo : (by + 1) * duo] = jnp.where(hit, 1.0, 0.0).astype(BF16)
+
+    def pick(group, part):
+        def put(cols, width):
+            seen = xa[:, :, cols].reshape(tokens, width)
+            picked = dot(pm[group], seen).astype(BF16)
             rh[c, group, bpos, :, cols] = picked[:duo]
             for i in range(3):
                 cs[group, i, :, cols] = picked[(i + 1) * duo : (i + 2) * duo]
 
-        @pl.loop(0, tiles)
-        def _(j):
-            cols = pl.ds(pl.multiple_of(j * tile, tile), tile)
-            put(cols, dot(pm[...], xa[:, :, cols].reshape(tokens, tile)).astype(BF16))
-
-        put(
-            pl.ds(half, META),
-            dot(pm[...], xa[:, :, half:].reshape(tokens, META)).astype(BF16),
-        )
+        start = (quarter, 0)[part]
+
+        for j in range(tiles):
+            put(pl.ds(start + j * tile, tile), tile)
+        if part == 0:
+            put(pl.ds(half, META), META)
         for index in (2, 0, 1):
-            send(group, index).start()
-        give(group, bpos, 0)
-
-    def send(group, index):
-        sem = group * 3 + index
+            send(group, index, part).start()
+
+    def send(group, index, part):
+        sem = (group * 2 + part) * 3 + index
+        cols = (ahead, behind)[part]
         copy = remote(
-            cs.at[group, moves[index] - 1],
-            rh.at[c, group, bpos],
+            cs.at[group, moves[index] - 1, :, cols],
+            rh.at[c, group, bpos, :, cols],
             csend.at[sem],
             crecv.at[sem],
             b_peers[index],
@@ -303,36 +337,50 @@
         return copy
 
     def give(group, place, index):
-        sem = 6 + group * 4 + index
+        sem = 12 + group * 4 + index
         ref = rh.at[c, group, place]
         copy = remote(ref, ref, csend.at[sem], crecv.at[sem], sib)
         copy.start()
         routed.append(copy)
 
-    pick(0)
-    pick(1)
-    sh.arrive()
-    sh.shared(lambda q: sa.at[d, q])
-    loads[4].wait()
-    total = jnp.zeros(sres.shape, F32)
-    wide = sa.shape[3]
-    for zz in range(RING):
-        for cc in range(2):
-            total += dot(sa[cc, zz], sd[(zz * 2 + cc) * wide : (zz * 2 + cc + 1) * wide, :])
-    sres[...] = total
+    choose(0)
+    pick(0, 0)
+    choose(1)
+    ring_end(1)
+    pick(0, 1)
+    give(0, bpos, 0)
+    pick(1, 0)
+    pick(1, 1)
+    give(1, bpos, 0)
+    for part, held in enumerate((za, zb)):
+        ref = held.at[d]
+        remote(ref, ref, zsend.at[14 + part], zrecv.at[14 + part], sib).wait_recv()
+    xo[:, quarter:] = normed(d, 0)
+    xo[:, :quarter] = normed(d, 1)
+
+    loads[0].wait()
+    loads[1].wait()
+    own_rows = pl.ds(pl.multiple_of(c * half, 128), half)
+    other_rows = pl.ds(pl.multiple_of(d * half, 128), half)
+    mine = xa[apos, :, :half]
+    s_gate = dot(mine, sg[own_rows, :]) + dot(xo[...], sg[other_rows, :])
+    s_up = dot(mine, su[own_rows, :]) + dot(xo[...], su[other_rows, :])
+    sa[c, z] = (s_gate / (1.0 + jnp.exp(-s_gate)) * s_up).astype(BF16)
+    sh = Gather(lambda q: sa.at[c, q], z, z_peers, ssend, srecv, sib)
+    sh.start()
     oo[:, :, 2 * duo : META] = jnp.zeros((2, 2, META - 2 * duo, oo.shape[3]), BF16)
     oo[:, :, META + 2 * duo :] = jnp.zeros((2, 2, META - 2 * duo, oo.shape[3]), BF16)
 
     def collect(group):
         for index, by in ((0, 3), (1, 1), (2, 2)):
-            sem = group * 3 + index
             place = step(bpos, by)
-            remote(
-                cs.at[group, 0], rh.at[c, group, place], csend.at[sem], crecv.at[sem], sib
-            ).wait_recv()
+            for part in range(2):
+                sem = (group * 2 + part) * 3 + index
+                ref = rh.at[c, group, place, :, (ahead, behind)[part]]
+                remote(ref, ref, csend.at[sem], crecv.at[sem], sib).wait_recv()
             give(group, place, index + 1)
         for index, by in ((0, 0), (1, 3), (2, 1), (3, 2)):
-            sem = 6 + group * 4 + index
+            sem = 12 + group * 4 + index
             ref = rh.at[d, group, step(apos, by)]
             remote(ref, ref, csend.at[sem], crecv.at[sem], sib).wait_recv()
 
@@ -365,27 +413,47 @@
             ac[c, z, group, slots:, i * META : (i + 1) * META] = column.T[:16].astype(BF16)
         ac[c, z, group, slots:, 2 * META :] = jnp.zeros((16, ac.shape[4] - 2 * META), BF16)
 
-        @pl.loop(0, wg.shape[1] // tile)
-        def _(j):
-            cols = pl.ds(pl.multiple_of(j * tile, tile), tile)
+        gathers = []
+        for j in range(wg.shape[1] // tile):
+            cols = pl.ds(j * tile, tile)
             one = rh[0, group, :, :, :half].reshape(slots, half)
             two = rh[1, group, :, :, :half].reshape(slots, half)
             g = dot(one, wg[:half, cols]) + turned(dot(two, wg[half:, cols]), group)
             u = dot(one, wu[:half, cols]) + turned(dot(two, wu[half:, cols]), group)
             ac[c, z, group, :slots, cols] = (g / (1.0 + jnp.exp(-g)) * u * factor).astype(BF16)
-
-        return Gather(
-            lambda q: ac.at[c, q, group], z, z_peers, gsend.at[group], grecv.at[group], sib
-        )
+            gather = Gather(
+                lambda q, cols=cols: ac.at[c, q, group, :, cols],
+                z,
+                z_peers,
+                gsend.at[group, j],
+                grecv.at[group, j],
+                sib,
+            )
+            gather.start()
+            gathers.append(gather)
+        return gathers
+
+    def hidden_in(group):
+        for gather in gg[group]:
+            gather.arrive()
+        for j, gather in enumerate(gg[group]):
+            gather.shared(lambda q: ac.at[d, q, group, :, pl.ds(j * tile, tile)])
 
     collect(0)
     loads[2].wait()
     loads[3].wait()
     gg = [hidden(0)]
-    gg[0].start()
     collect(1)
     gg.append(hidden(1))
-    gg[1].start()
+    sh.arrive()
+    sh.shared(lambda q: sa.at[d, q])
+    loads[4].wait()
+    total = jnp.zeros(sres.shape, F32)
+    wide = sa.shape[3]
+    for zz in range(RING):
+        for cc in range(2):
+            total += dot(sa[cc, zz], sd[(zz * 2 + cc) * wide : (zz * 2 + cc + 1) * wide, :])
+    sres[...] = total
 
     width = oo.shape[3]
     deep = ac.shape[4]
@@ -456,13 +524,11 @@
             for k in range(2):
                 t1[h, 2 * k + lax.rem(pos + group, 2)] = whole[k].astype(BF16)
 
-    gg[0].arrive()
-    gg[0].shared(lambda q: ac.at[d, q, 0])
+    hidden_in(0)
     loads[5].wait()
     outputs(0)
     spread_first(0)
-    gg[1].arrive()
-    gg[1].shared(lambda q: ac.at[d, q, 1])
+    hidden_in(1)
     outputs(1)
     spread_first(1)
     sum_first(0)
@@ -480,8 +546,15 @@
             )
             copy.start()
             sums2.append(copy)
-    cols = pl.ds(pl.multiple_of(lax.rem(local, RING) * width, 128), width)
-    left = zh[z // 2, :, :, cols].reshape(block, width).astype(F32) + sres[...]
+    fore = spread_out(za[z // 2, :, :, :eighth])
+    aft = spread_out(zb[z // 2])
+    late = lax.rem(z, 2) == 1
+    left = jnp.where(
+        late,
+        jnp.where(c == 0, fore[0], fore[1]),
+        jnp.where(c == 0, aft[0], aft[1]),
+    )
+    left = left + sres[...]
     for h in range(2):
         pos = axes[1 - h][0]
         whole = left[h * ht : (h + 1) * ht] + t1[h, pos].astype(F32)
@@ -490,9 +563,9 @@
             whole += r2[h, index].astype(F32)
         out[h * ht : (h + 1) * ht] = whole.astype(BF16)
 
-    for gather in [zg, sh] + gg:
+    for gather in [sh] + gg[0] + gg[1]:
         gather.drain()
-    for copy in around + routed + sums1 + sums2:
+    for copy in first + around + routed + sums1 + sums2:
         copy.wait_send()
 
 
@@ -521,13 +594,14 @@
             pltpu.VMEM(sgate.shape, BF16),
             pltpu.VMEM(sup.shape, BF16),
             pltpu.VMEM(sdown.shape, BF16),
-            pltpu.VMEM((rows, half + META), F32),
-            pltpu.VMEM((rows, half + META), F32),
-            pltpu.VMEM((2, RING, 2 * rows, half + META), BF16),
+            pltpu.VMEM((2 * rows, half // 4 + META), BF16),
+            pltpu.VMEM((2 * rows, half // 4), BF16),
+            pltpu.VMEM((2, 2 * RING, 2 * rows, half // 4 + META), BF16),
+            pltpu.VMEM((2, 2 * RING, 2 * rows, half // 4), BF16),
             pltpu.VMEM((RING, block, half + META), BF16),
             pltpu.VMEM((block, half), BF16),
             pltpu.VMEM((META, RING * block), F32),
-            pltpu.VMEM((slots, RING * block), BF16),
+            pltpu.VMEM((2, slots, RING * block), BF16),
             pltpu.VMEM((2, 3, duo, half + META), BF16),
             pltpu.VMEM((2, 2, RING, duo, half + META), BF16),
             pltpu.VMEM((2, RING, 2, slots + 16, units), BF16),
@@ -539,17 +613,16 @@
             pltpu.VMEM((2, 3, ht, cols), BF16),
             pltpu.VMEM((2, RING, ht, cols), BF16),
             dma((6,)),
-            dma((2,)),
+            dma((16,)),
+            dma((16,)),
+            dma((12,)),
+            dma((12,)),
             dma((7,)),
             dma((7,)),
-            dma((6,)),
-            dma((6,)),
-            dma((7,)),
-            dma((7,)),
-            dma((14,)),
-            dma((14,)),
-            dma((2, 7)),
-            dma((2, 7)),
+            dma((20,)),
+            dma((20,)),
+            dma((2, 2, 7)),
+            dma((2, 2, 7)),
             dma((18,)),
             dma((18,)),
         ],

time: 86.3 us -> 79 us (0.915)
  Pallas kernels: 84.6 us -> 77.3 us
    pallas_call x1, Pallas kernels: 84.6 us -> 77.3 us  [body(): pl.pallas_call(kernel, out_shape=jax.ShapeDtypeStruct((block, cols), BF16...]
where the time goes in v3:
time: 79 us; the launch traced here: 78.9 us
  Pallas kernels  77.3 us (98%)
  local copies, waits for them, and re-layouts  1.55 us (2%)
    pallas_call x1, Pallas kernels, body(): pl.pallas_call(kernel, out_shape=jax.ShapeDtypeStruct((block, cols), BF16...  77.3 us

profile of v3, /device:TPU:0, one launch (start us, length us, event | category | flops | bytes accessed | tf_op | source)
XLA Modules:
  0.0 78.9 jit_solution(2486609659464380274)
XLA Ops:
  0.0 77.3 %shard_map.100 = bf16[64,896]{1,0:T(8,128)(2,1)} custom-call(bf16[8,7168]{1,0:T(8,128)(2,1)} %hid.1, s32[8,8]{1,0:T(8,128)} %ids.1, bf16[8,8]{1,0:T(8,128)(2,1)} %aff.1, f32[2,1,3584]{2,1,0:T(1,128)} %bitcast.1, bf16[1,7168,512]{2,1,0:T(8,128)(2,1)} %gate_hbm.1, bf16[1,7168,512]{2,1,0:T(8,128)(2,1)} %up_hbm.1, bf16[2,2048,896]{2,1,0:T(8,128)(2,1)} %down_hbm.1, ...), custom_call_target="tpu_custom_call" | custom-call | tf_op jit(solution)/shard_map/pallas_call | solution.py:585
  77.3 1.6 %copy.12 = bf16[64,896]{1,0:T(8,128)(2,1)} copy(bf16[64,896]{1,0:T(8,128)(2,1)} %shard_map.100) | data formatting | bytes 229376

commit v4 on v3

--- a/solution.py
+++ b/solution.py
@@ -60,16 +60,21 @@
         for index, origin in enumerate([self.pos] + self.origins):
             self.copy(mirror(origin), 3 + index, self.other).wait_recv()
 
+    def settle(self):
+        for copy in self.sent[:3]:
+            copy.wait_send()
+        self.sent = self.sent[3:]
+
     def drain(self):
         for copy in self.sent:
             copy.wait_send()
 
 
 def kernel(
-    hid,
-    ids,
-    aff,
-    gain,
+    hid_hbm,
+    ids_hbm,
+    aff_hbm,
+    gain_hbm,
     gate_hbm,
     up_hbm,
     down_hbm,
@@ -77,6 +82,10 @@
     sup_hbm,
     sdown_hbm,
     out,
+    hid,
+    ids,
+    aff,
+    gain,
     wg,
     wu,
     wd,
@@ -96,6 +105,7 @@
     ac,
     sa,
     sres,
+    acc,
     oo,
     pp,
     r1,
@@ -136,6 +146,17 @@
     for peer in everyone:
         pl.semaphore_signal(barrier, inc=1, device_id=peer, device_id_type=MESH)
 
+    little = [
+        pltpu.make_async_copy(src, dst, wsem.at[6 + i])
+        for i, (src, dst) in enumerate(
+            ((hid_hbm, hid), (ids_hbm, ids), (aff_hbm, aff), (gain_hbm, gain))
+        )
+    ]
+    for load in little:
+        load.start()
+    for load in little:
+        load.wait()
+
     values = hid[...].astype(F32)
     scale = lax.rsqrt(jnp.mean(values * values, axis=-1, keepdims=True) + 1e-06)
     s_hi = scale.astype(BF16).astype(F32)
@@ -173,8 +194,9 @@
     pa[:, eighth:] = beside
     pb[...] = laid(d, 0).astype(BF16)
     pl.semaphore_wait(barrier, len(everyone))
-    first = []
-    for part, (mine, other, held) in enumerate(((za.at[c, local], pa, za), (zb.at[c, local], pb, zb))):
+    def hand_out(part):
+        mine, other, held = ((za.at[c, local], pa, za), (zb.at[c, local], pb, zb))[part]
+        batch = []
         for index, device in enumerate(z_peers + z_cross + [sib]):
             whose = c if index < 3 else d
             sem = part * 7 + index
@@ -186,7 +208,13 @@
                 device,
             )
             copy.start()
-            first.append(copy)
+            batch.append(copy)
+        return batch
+
+    def sent(batch):
+        for copy in batch:
+            copy.wait_send()
+
     loads = [
         pltpu.make_async_copy(src, dst, wsem.at[i])
         for i, (src, dst) in enumerate(
@@ -200,6 +228,9 @@
             )
         )
     ]
+    batch = hand_out(0)
+    sent(batch)
+    first = hand_out(1)
     for load in loads:
         load.start()
 
@@ -248,9 +279,16 @@
         copy.start()
         around.append(copy)
 
-    def ring_start(part):
-        go(ring(part, apos, upper, 0, a_peers[0]))
-        go(ring(part, apos, lower, 1, a_peers[1]))
+    def ring_first(part):
+        batch = [
+            ring(part, apos, upper, 0, a_peers[0]),
+            ring(part, apos, lower, 1, a_peers[1]),
+        ]
+        for copy in batch:
+            copy.start()
+        return batch
+
+    def ring_second(part):
         go(ring(part, apos, lower, 2, a_peers[0]))
         go(ring(part, apos, upper, 3, a_peers[1]))
 
@@ -269,13 +307,17 @@
     share = gathered(0)
     xa[apos, :, quarter:half] = normed(c, 0)
     xa[apos, :, half:] = spread_out(za[c, :, :, eighth:])[0].astype(BF16)
-    ring_start(0)
+    batch = ring_first(0)
     share.start()
+    sent(batch)
+    ring_second(0)
     share = gathered(1)
     xa[apos, :, :quarter] = normed(c, 1)
-    ring_start(1)
+    batch = ring_first(1)
     share.start()
     ring_on(0)
+    sent(batch)
+    ring_second(1)
     ring_on(1)
     ring_end(0)
 
@@ -294,7 +336,6 @@
 
     duo = 2 * CAP
     tile = 256
-    tiles = quarter // tile
     slot_no = lax.broadcasted_iota(jnp.int32, (duo, tokens), 0).astype(F32)
     parity = lax.rem(lax.broadcasted_iota(jnp.int32, (duo, tokens), 1) // block, 2)
     routed = []
@@ -316,12 +357,14 @@
 
         start = (quarter, 0)[part]
 
-        for j in range(tiles):
-            put(pl.ds(start + j * tile, tile), tile)
+        put(pl.ds(start, quarter), quarter)
         if part == 0:
             put(pl.ds(half, META), META)
-        for index in (2, 0, 1):
-            send(group, index, part).start()
+    def send_all(group, part):
+        batch = [send(group, index, part) for index in (2, 0, 1)]
+        for copy in batch:
+            copy.start()
+        return batch
 
     def send(group, index, part):
         sem = (group * 2 + part) * 3 + index
@@ -333,25 +376,29 @@
             crecv.at[sem],
             b_peers[index],
         )
-        routed.append(copy)
         return copy
 
-    def give(group, place, index):
-        sem = 12 + group * 4 + index
-        ref = rh.at[c, group, place]
-        copy = remote(ref, ref, csend.at[sem], crecv.at[sem], sib)
+    def kept(h, group, place, part, index):
+        sem = 12 + (group * 2 + part) * 4 + index
+        ref = rh.at[h, group, place, :, (ahead, behind)[part]]
+        return remote(ref, ref, csend.at[sem], crecv.at[sem], sib)
+
+    def give(group, place, part, index):
+        copy = kept(c, group, place, part, index)
         copy.start()
         routed.append(copy)
 
     choose(0)
     pick(0, 0)
+    batches = [send_all(0, 0)]
+    give(0, bpos, 0, 0)
     choose(1)
     ring_end(1)
     pick(0, 1)
-    give(0, bpos, 0)
+    batches.append(send_all(0, 1))
+    give(0, bpos, 1, 0)
     pick(1, 0)
     pick(1, 1)
-    give(1, bpos, 0)
     for part, held in enumerate((za, zb)):
         ref = held.at[d]
         remote(ref, ref, zsend.at[14 + part], zrecv.at[14 + part], sib).wait_recv()
@@ -368,21 +415,24 @@
     sa[c, z] = (s_gate / (1.0 + jnp.exp(-s_gate)) * s_up).astype(BF16)
     sh = Gather(lambda q: sa.at[c, q], z, z_peers, ssend, srecv, sib)
     sh.start()
+    for part in range(2):
+        sent(batches[part])
+        routed += send_all(1, part)
+        give(1, bpos, part, 0)
     oo[:, :, 2 * duo : META] = jnp.zeros((2, 2, META - 2 * duo, oo.shape[3]), BF16)
     oo[:, :, META + 2 * duo :] = jnp.zeros((2, 2, META - 2 * duo, oo.shape[3]), BF16)
 
     def collect(group):
-        for index, by in ((0, 3), (1, 1), (2, 2)):
-            place = step(bpos, by)
-            for part in range(2):
+        for part in range(2):
+            for index, by in ((0, 3), (1, 1), (2, 2)):
+                place = step(bpos, by)
                 sem = (group * 2 + part) * 3 + index
                 ref = rh.at[c, group, place, :, (ahead, behind)[part]]
                 remote(ref, ref, csend.at[sem], crecv.at[sem], sib).wait_recv()
-            give(group, place, index + 1)
-        for index, by in ((0, 0), (1, 3), (2, 1), (3, 2)):
-            sem = 12 + group * 4 + index
-            ref = rh.at[d, group, step(apos, by)]
-            remote(ref, ref, csend.at[sem], crecv.at[sem], sib).wait_recv()
+                give(group, place, part, index + 1)
+        for part in range(2):
+            for index, by in ((0, 0), (1, 3), (2, 1), (3, 2)):
+                kept(d, group, step(apos, by), part, index).wait_recv()
 
     slots = RING * duo
     expert = (node * 2 + z // 2).astype(F32)
@@ -429,15 +479,11 @@
                 grecv.at[group, j],
                 sib,
             )
+            if group == 1:
+                gg[0][j].settle()
             gather.start()
             gathers.append(gather)
         return gathers
-
-    def hidden_in(group):
-        for gather in gg[group]:
-            gather.arrive()
-        for j, gather in enumerate(gg[group]):
-            gather.shared(lambda q: ac.at[d, q, group, :, pl.ds(j * tile, tile)])
 
     collect(0)
     loads[2].wait()
@@ -445,37 +491,34 @@
     gg = [hidden(0)]
     collect(1)
     gg.append(hidden(1))
-    sh.arrive()
-    sh.shared(lambda q: sa.at[d, q])
-    loads[4].wait()
-    total = jnp.zeros(sres.shape, F32)
-    wide = sa.shape[3]
-    for zz in range(RING):
-        for cc in range(2):
-            total += dot(sa[cc, zz], sd[(zz * 2 + cc) * wide : (zz * 2 + cc + 1) * wide, :])
-    sres[...] = total
-
     width = oo.shape[3]
     deep = ac.shape[4]
     ht = block // 2
     row_no = lax.broadcasted_iota(jnp.int32, (tokens, META), 0).astype(F32)
 
-    def outputs(group):
+    def outputs(group, j):
+        gg[group][j].arrive()
+        gg[group][j].shared(lambda q: ac.at[d, q, group, :, pl.ds(j * tile, tile)])
         for e in range(2):
             for lo in range(0, width, tile):
                 hi = min(lo + tile, width)
-                res = jnp.zeros((slots, hi - lo), F32)
+                res = jnp.zeros((slots, hi - lo), F32) if j == 0 else acc[e, :, lo:hi]
                 for zz in range(2):
                     for cc in range(2):
-                        k = zz * 2 + cc
+                        at = (zz * 2 + cc) * deep + j * tile
                         res += dot(
-                            ac[cc, e * 2 + zz, group, :slots, :],
-                            wd[e, k * deep : (k + 1) * deep, lo:hi],
+                            ac[cc, e * 2 + zz, group, :slots, j * tile : (j + 1) * tile],
+                            wd[e, at : at + tile, lo:hi],
                         )
+                if j == 0:
+                    acc[e, :, lo:hi] = res
+                    continue
                 for i in range(2):
                     oo[group, i, e * META : e * META + 2 * duo, lo:hi] = res[
                         i * 2 * duo : (i + 1) * 2 * duo
                     ].astype(BF16)
+
+    def combine(group):
         for i in range(2):
             spread = [
                 jnp.where(
@@ -524,12 +567,24 @@
             for k in range(2):
                 t1[h, 2 * k + lax.rem(pos + group, 2)] = whole[k].astype(BF16)
 
-    hidden_in(0)
     loads[5].wait()
-    outputs(0)
+    outputs(0, 0)
+    outputs(0, 1)
+    combine(0)
     spread_first(0)
-    hidden_in(1)
-    outputs(1)
+    sh.arrive()
+    sh.shared(lambda q: sa.at[d, q])
+    loads[4].wait()
+    total = jnp.zeros(sres.shape, F32)
+    wide = sa.shape[3]
+    for zz in range(RING):
+        for cc in range(2):
+            total += dot(sa[cc, zz], sd[(zz * 2 + cc) * wide : (zz * 2 + cc + 1) * wide, :])
+    sres[...] = total
+
+    outputs(1, 0)
+    outputs(1, 1)
+    combine(1)
     spread_first(1)
     sum_first(0)
     sum_first(1)
@@ -585,9 +640,13 @@
     return pl.pallas_call(
         kernel,
         out_shape=jax.ShapeDtypeStruct((block, cols), BF16),
-        in_specs=[vmem] * 4 + [hbm] * 6,
+        in_specs=[hbm] * 10,
         out_specs=vmem,
         scratch_shapes=[
+            pltpu.VMEM(hid.shape, BF16),
+            pltpu.VMEM(ids.shape, jnp.int32),
+            pltpu.VMEM(aff.shape, BF16),
+            pltpu.VMEM((2, 1, half), F32),
             pltpu.VMEM((width, units), BF16),
             pltpu.VMEM((width, units), BF16),
             pltpu.VMEM(down.shape, BF16),
@@ -607,20 +666,21 @@
             pltpu.VMEM((2, RING, 2, slots + 16, units), BF16),
             pltpu.VMEM((2, RING, block, shared), BF16),
             pltpu.VMEM((block, cols), F32),
+            pltpu.VMEM((2, slots, cols), F32),
             pltpu.VMEM((2, 2, 2 * META, cols), BF16),
             pltpu.VMEM((2, 2, RING, 2, ht, cols), BF16),
             pltpu.VMEM((2, 2, 3, 2, ht, cols), BF16),
             pltpu.VMEM((2, 3, ht, cols), BF16),
             pltpu.VMEM((2, RING, ht, cols), BF16),
-            dma((6,)),
+            dma((10,)),
             dma((16,)),
             dma((16,)),
             dma((12,)),
             dma((12,)),
             dma((7,)),
             dma((7,)),
-            dma((20,)),
-            dma((20,)),
+            dma((28,)),
+            dma((28,)),
             dma((2, 2, 7)),
             dma((2, 2, 7)),
             dma((18,)),

time: 79 us -> 76.3 us (0.966)
  Pallas kernels: 77.3 us -> 74.6 us
    pallas_call x1, Pallas kernels: 77.3 us -> 74.6 us  [body(): pl.pallas_call(kernel, out_shape=jax.ShapeDtypeStruct((block, cols), BF16...]
where the time goes in v4:
time: 76.3 us; the launch traced here: 76.1 us
  Pallas kernels  74.6 us (98%)
  local copies, waits for them, and re-layouts  1.55 us (2%)
    pallas_call x1, Pallas kernels, body(): pl.pallas_call(kernel, out_shape=jax.ShapeDtypeStruct((block, cols), BF16...  74.6 us
    unnamed x1, local copies, waits for them, and re-layouts  1.55 us

profile of v4, /device:TPU:0, one launch (start us, length us, event | category | flops | bytes accessed | tf_op | source)
XLA Modules:
  0.0 76.1 jit_solution(5777839810090869560)
XLA Ops:
  0.0 74.6 %shard_map.100 = bf16[64,896]{1,0:T(8,128)(2,1)} custom-call(bf16[8,7168]{1,0:T(8,128)(2,1)} %hid_hbm.1, s32[8,8]{1,0:T(8,128)} %ids_hbm.1, bf16[8,8]{1,0:T(8,128)(2,1)} %aff_hbm.1, f32[2,1,3584]{2,1,0:T(1,128)} %bitcast.1, bf16[1,7168,512]{2,1,0:T(8,128)(2,1)} %gate_hbm.1, bf16[1,7168,512]{2,1,0:T(8,128)(2,1)} %up_hbm.1, bf16[2,2048,896]{2,1,0:T(8,128)(2,1)} %down_hbm.1, ...), custom_call_target="tpu_custom_call" | custom-call | tf_op jit(solution)/shard_map/pallas_call | solution.py:640
  74.6 1.6 %copy.12 = bf16[64,896]{1,0:T(8,128)(2,1)} copy(bf16[64,896]{1,0:T(8,128)(2,1)} %shard_map.100) | data formatting | bytes 229376

commit v5 on v4

--- a/solution.py
+++ b/solution.py
@@ -59,11 +59,6 @@
     def shared(self, mirror):
         for index, origin in enumerate([self.pos] + self.origins):
             self.copy(mirror(origin), 3 + index, self.other).wait_recv()
-
-    def settle(self):
-        for copy in self.sent[:3]:
-            copy.wait_send()
-        self.sent = self.sent[3:]
 
     def drain(self):
         for copy in self.sent:
@@ -479,8 +474,6 @@
                 grecv.at[group, j],
                 sib,
             )
-            if group == 1:
-                gg[0][j].settle()
             gather.start()
             gathers.append(gather)
         return gathers

time: 76.3 us -> 75.9 us (level)
  no operation moved by 1% of the time
where the time goes in v5:
time: 75.9 us; the launch traced here: 75.8 us
  Pallas kernels  74.2 us (98%)
  local copies, waits for them, and re-layouts  1.55 us (2%)
    pallas_call x1, Pallas kernels, body(): pl.pallas_call(kernel, out_shape=jax.ShapeDtypeStruct((block, cols), BF16...  74.2 us
    unnamed x1, local copies, waits for them, and re-layouts  1.55 us

profile of v5, /device:TPU:0, one launch (start us, length us, event | category | flops | bytes accessed | tf_op | source)
XLA Modules:
  0.0 75.8 jit_solution(1992917509175868618)
XLA Ops:
  0.0 74.2 %shard_map.100 = bf16[64,896]{1,0:T(8,128)(2,1)} custom-call(bf16[8,7168]{1,0:T(8,128)(2,1)} %hid_hbm.1, s32[8,8]{1,0:T(8,128)} %ids_hbm.1, bf16[8,8]{1,0:T(8,128)(2,1)} %aff_hbm.1, f32[2,1,3584]{2,1,0:T(1,128)} %bitcast.1, bf16[1,7168,512]{2,1,0:T(8,128)(2,1)} %gate_hbm.1, bf16[1,7168,512]{2,1,0:T(8,128)(2,1)} %up_hbm.1, bf16[2,2048,896]{2,1,0:T(8,128)(2,1)} %down_hbm.1, ...), custom_call_target="tpu_custom_call" | custom-call | tf_op jit(solution)/shard_map/pallas_call | solution.py:633
  74.2 1.6 %copy.12 = bf16[64,896]{1,0:T(8,128)(2,1)} copy(bf16[64,896]{1,0:T(8,128)(2,1)} %shard_map.100) | data formatting | bytes 229376
